TPU v7x, 32 devices: a whole 2x2x4 slice. The times are simulated.
32 devices in a mesh: parts: 2 (over x), store: 8 (over z, y), head: 2 (over core).
Axes of the slice: x: 2, y: 2, z: 4, core: 2. Of those that a mesh axis runs over, the one named last changes fastest.
Arguments:
- queries: bfloat16 [128, 64, 8192], P(('parts', 'store'), None, 'head'), parts along dimension 0, may hold values from -5 to 5, as said below
- own_keys: bfloat16 [128, 64, 1024], P(('parts', 'store'), None, 'head'), parts along dimension 0, may hold values from -5 to 5, as said below
- own_values: bfloat16 [128, 64, 1024], P(('parts', 'store'), None, 'head'), parts along dimension 0, may hold values from -6 to 6
- passage_kv: bfloat16 [768, 2, 32, 1024], P(('parts', 'store', 'head')), parts along dimension 0, may hold values from -6 to 6
- passage_rows: int32 [768], P('parts'), parts along dimension 0, may hold values from 0 to 383, as said below
- retrieval: int32 [128, 16], P(('parts', 'store')), parts along dimension 0, may hold values from 0 to 383, as said below
- offsets: int32 [768], P('parts'), parts along dimension 0, may hold values from 0 to 2047
Outputs:
- attended: bfloat16 [128, 64, 8192], P(('parts', 'store'), None, 'head'), parts along dimension 0
There are 2 independent parts, one for each index of `parts`. A program takes and returns all parts, laid end to end along the dimension named above; each array names one. Nothing has to cross between parts.
Inputs may be any that keep to these rules, and one draw needn't show every extreme that they name: queries have entries of order one. own_keys have entries of order one. `passage_rows`: A permutation of the passage ids. `retrieval`: each request names 16 different passages, and the 8 requests of one aligned block (one request group) name no passage twice. Among those 128 passages, at most 12 have their row on one device of the store (row // 24), and some device holds exactly 12 of them.
All inputs are finite; a program needn't handle non-finite values.
Results may differ from a plain program's by a relative error of at most 0.0059.
Values may be sent and summed in bfloat16 or wider, within the bound.
A program may use at most 128 MiB of HBM per device.

v0:
```python
import jax
import jax.numpy as jnp
from jax import lax
from jax.sharding import PartitionSpec as P

HEAD_DIM = 128
NPASS = 16
PLEN = 32


rope_theta = 1000000.0


def rerotate(page_keys, turn_by):
    count, length, width = page_keys.shape
    half_dim = HEAD_DIM // 2
    spread = page_keys.astype(jnp.float32).reshape(count, length, width // HEAD_DIM, HEAD_DIM)
    first_half = spread[..., :half_dim]
    second_half = spread[..., half_dim:]
    inverse_freq = rope_theta ** (-(jnp.arange(half_dim, dtype=jnp.float32) * 2.0) / HEAD_DIM)
    angles = turn_by.astype(jnp.float32)[:, None] * inverse_freq[None, :]
    cosine = jnp.cos(angles)[:, None, None, :]
    sine_vals = jnp.sin(angles)[:, None, None, :]
    turned = jnp.concatenate(
        [
            first_half * cosine - second_half * sine_vals,
            second_half * cosine + first_half * sine_vals,
        ],
        axis=-1,
    )
    return turned.reshape(count, length, width).astype(jnp.bfloat16)


def attend(question, key_rows, value_rows):
    qlen_here = question.shape[0]
    key_count = key_rows.shape[0]
    query_heads = question.shape[1] // HEAD_DIM
    kv_count = key_rows.shape[1] // HEAD_DIM
    group = query_heads // kv_count
    by_head = (
        question.reshape(qlen_here, kv_count, group, HEAD_DIM)
        .transpose(1, 2, 0, 3)
        .reshape(kv_count, group * qlen_here, HEAD_DIM)
    )
    key_heads = key_rows.reshape(key_count, kv_count, HEAD_DIM).transpose(1, 0, 2)
    value_heads = value_rows.reshape(key_count, kv_count, HEAD_DIM).transpose(1, 0, 2)
    row_pos = jnp.tile(jnp.arange(qlen_here), group)
    own_pos = jnp.arange(key_count) - (key_count - qlen_here)
    visible = own_pos[None, :] <= row_pos[:, None]

    def one_head(triple):
        query_block, key_block, value_block = triple
        scores = jnp.dot(
            query_block, key_block.T, preferred_element_type=jnp.float32
        ) * HEAD_DIM ** (-0.5)
        scores = jnp.where(visible, scores, -jnp.inf)
        peak = jnp.max(scores, axis=1, keepdims=True)
        expo = jnp.exp(scores - peak)
        weights = (expo / jnp.sum(expo, axis=1, keepdims=True)).astype(jnp.bfloat16)
        return jnp.dot(weights, value_block, preferred_element_type=jnp.float32).astype(
            jnp.bfloat16
        )

    result = lax.map(one_head, (by_head, key_heads, value_heads))
    return (
        result.reshape(kv_count, group, qlen_here, HEAD_DIM)
        .transpose(2, 0, 1, 3)
        .reshape(qlen_here, query_heads * HEAD_DIM)
    )


def ranks_within(owner_ids):
    count = owner_ids.shape[0]
    same_owner = owner_ids[:, None] == owner_ids[None, :]
    earlier = jnp.arange(count)[None, :] < jnp.arange(count)[:, None]
    return jnp.sum(same_owner & earlier, axis=1)


def request_table(slot_index, local_row, total):
    hits = slot_index[:, None] == jnp.arange(total)[None, :]
    return jnp.sum(jnp.where(hits, local_row[:, None], 0), axis=0)


def local(queries, own_keys, own_values, passage_kv, passage_rows, retrieval, offsets):
    stored_count = passage_kv.shape[0]
    half_width = passage_kv.shape[3] // 2
    store_count = lax.axis_size("store")
    head_count = lax.axis_size("head")
    peer_count = store_count * head_count
    pick_ids = retrieval.reshape(-1)
    pick_count = pick_ids.shape[0]
    cap_dev = 3 * pick_count // (2 * peer_count)
    store_rows = passage_rows[pick_ids]
    pick_index = jnp.arange(pick_count, dtype=jnp.int32)
    owner_dev = store_rows // stored_count
    local_row = store_rows % stored_count
    slot_index = owner_dev * cap_dev + ranks_within(owner_dev)
    asked = request_table(slot_index, local_row, peer_count * cap_dev).reshape(peer_count, cap_dev)
    wanted = lax.all_to_all(asked, ("store", "head"), split_axis=0, concat_axis=0, tiled=True)
    split_store = passage_kv.reshape(stored_count, 2, PLEN, head_count, half_width).transpose(
        0, 3, 1, 2, 4
    )
    split_store = split_store.reshape(stored_count * head_count, 2, PLEN, half_width)
    half_index = jnp.arange(peer_count, dtype=jnp.int32) % head_count
    outgoing = split_store[wanted * head_count + half_index[:, None]]
    incoming = lax.all_to_all(outgoing, ("store", "head"), split_axis=0, concat_axis=0, tiled=True)
    fetched = incoming.reshape(peer_count * cap_dev, 2, PLEN, half_width)[slot_index]
    turn_by = pick_index % NPASS * PLEN - offsets[pick_ids]
    moved = rerotate(fetched[:, 0], turn_by)
    request_count = queries.shape[0]
    key_rows = jnp.concatenate(
        [moved.reshape(request_count, NPASS * PLEN, half_width), own_keys], axis=1
    )
    value_rows = jnp.concatenate(
        [fetched[:, 1].reshape(request_count, NPASS * PLEN, half_width), own_values], axis=1
    )

    def one_request(triple):
        return attend(triple[0], triple[1], triple[2])

    return lax.map(one_request, (queries, key_rows, value_rows))


def solution(mesh):
    in_specs = (
        P(("parts", "store"), None, "head"),
        P(("parts", "store"), None, "head"),
        P(("parts", "store"), None, "head"),
        P(("parts", "store", "head"), None, None, None),
        P("parts"),
        P(("parts", "store"), None),
        P("parts"),
    )
    out_specs = P(("parts", "store"), None, "head")
    return jax.shard_map(local, mesh=mesh, in_specs=in_specs, out_specs=out_specs, check_vma=False)
```

profile of v0, /device:TPU:15, one launch (start us, length us, event | category | flops | bytes accessed | tf_op | source)
XLA Modules:
  0.0 434.5 jit_solution(15516422699108855504)
XLA Ops:
  3.1 6.6 %all-to-all-start = ((s32[16,1,12]{2,1,0:T(1,128)}), s32[16,1,12]{2,1,0:T(1,128)S(1)}, u32[]{:S(2)}, u32[]{:S(2)}) async-start(s32[16,1,12]{2,1,0:T(1,128)} %bitcast.8), calls=%async_computation | async-start | bytes 16384 | tf_op jit(solution)/shard_map/all_to_all | solution.py:99
  9.7 2.1 fusion.24
  12.1 1.3 all-to-all-done
  13.6 8.2 %gather_fusion.1 = bf16[192,2,32,512]{3,2,1,0:T(8,128)(2,1)} fusion(bf16[48,2,32,512]{3,2,1,0:T(8,128)(2,1)S(1)} %bitcast.85, s32[1024]{0:T(1024)S(1)} %pad_clamp_fusion.1), kind=kCustom, calls=%fused_computation.1 | custom fusion | bytes 25166592 | tf_op jit(solution)/shard_map/gather | solution.py:105
  21.8 7.5 %all-to-all-start.1 = ((bf16[16,12,2,32,512]{4,3,2,1,0:T(8,128)(2,1)}), bf16[16,12,2,32,512]{4,3,2,1,0:T(8,128)(2,1)}, u32[]{:S(2)}, u32[]{:S(2)}) async-start(bf16[16,12,2,32,512]{4,3,2,1,0:T(8,128)(2,1)} %bitcast.90), calls=%async_computation.1 | async-start | bytes 25165824 | tf_op jit(solution)/shard_map/all_to_all | solution.py:106
  31.0 270.6 %all-to-all-done.1 = bf16[16,12,2,32,512]{4,3,2,1,0:T(8,128)(2,1)} async-done(((bf16[16,12,2,32,512]{4,3,2,1,0:T(8,128)(2,1)}), bf16[16,12,2,32,512]{4,3,2,1,0:T(8,128)(2,1)}, u32[]{:S(2)}, u32[]{:S(2)}) %all-to-all-start.1) | async-done | bytes 12582944 | tf_op jit(solution)/shard_map/all_to_all | solution.py:106
  301.6 11.1 %gather_fusion.2 = bf16[128,2,32,512]{3,2,1,0:T(8,128)(2,1)} fusion(bf16[192,2,32,512]{3,2,1,0:T(8,128)(2,1)} %bitcast.11, s32[1024]{0:T(1024)S(1)} %pad_clamp_fusion), kind=kCustom, calls=%fused_computation.2 | custom fusion | bytes 16777728 | tf_op jit(solution)/shard_map/gather | solution.py:107
  312.7 7.7 %fusion.23 = (bf16[128,1,32,512]{3,2,1,0:T(8,128)(2,1)}, f32[128,1,32,512]{3,2,1,0:T(8,128)}) fusion(bf16[128,2,32,512]{3,2,1,0:T(8,128)(2,1)} %gather_fusion.2), kind=kLoop, calls=%fused_computation.65 | loop fusion | flops 2097152 | bytes 20971520 | tf_op jit(solution)/shard_map/slice | solution.py:115
  320.4 9.9 %reshape.296 = f32[128,32,4,128]{3,2,1,0:T(4,128)} reshape(f32[128,1,32,512]{3,2,1,0:T(8,128)} %get-tuple-element.182) | data formatting | bytes 16777216 | tf_op jit(solution)/shard_map/convert_element_type | solution.py:17
  330.3 11.0 %subtract_convert_fusion = (bf16[128,32,4,64]{3,2,1,0:T(4,128)(2,1)S(1)}, bf16[128,32,4,64]{3,2,1,0:T(4,128)(2,1)S(1)}) fusion(f32[128,32,4,128]{3,2,1,0:T(4,128)} %reshape.296, f32[128,64]{1,0:T(8,128)S(1)} %get-tuple-element.186, f32[128,64]{1,0:T(8,128)S(1)} %get-tuple-element.185), kind=kLoop, calls=%fused_computation.28 | loop fusion | flops 8388608 | bytes 12648448 | tf_op jit(solution)/shard_map/convert.1
  341.3 6.7 %pad_maximum_fusion.2 = bf16[128,32,4,128]{3,2,1,0:T(4,128)(2,1)} fusion(bf16[128,32,4,64]{3,2,1,0:T(4,128)(2,1)S(1)} %get-tuple-element.180, bf16[128,32,4,64]{3,2,1,0:T(4,128)(2,1)S(1)} %get-tuple-element.179), kind=kLoop, calls=%fused_computation.32 | loop fusion | flops 8388608 | bytes 8388608 | tf_op jit(solution)/shard_map/concatenate | solution.py:24
  348.0 7.3 %convert_element_type.32 = bf16[8,512,512]{2,1,0:T(8,128)(2,1)} reshape(bf16[128,32,4,128]{3,2,1,0:T(4,128)(2,1)} %pad_maximum_fusion.2) | data formatting | bytes 8388608 | tf_op jit(solution)/shard_map/convert_element_type | solution.py:31
  355.4 8.9 %pad_maximum_fusion = (bf16[8,576,512]{2,1,0:T(8,128)(2,1)}, bf16[8,576,512]{2,1,0:T(8,128)(2,1)}) fusion(bf16[8,64,512]{2,1,0:T(8,128)(2,1)S(1)} %copy-done.3, bf16[8,512,512]{2,1,0:T(8,128)(2,1)} %convert_element_type.32, bf16[8,64,512]{2,1,0:T(8,128)(2,1)S(1)} %copy-done.4, bf16[8,512,512]{2,1,0:T(8,128)(2,1)} %bitcast.91), kind=kLoop, calls=%fused_computation.29 | loop fusion | flops 18874368 | bytes 18874368 | tf_op jit(solution)/shard_map/concatenate | solution.py:111
  364.2 69.6 %while.33 = (s32[]{:T(128)}, bf16[8,64,4096]{2,1,0:T(8,128)(2,1)}, bf16[8,64,4096]{2,1,0:T(8,128)(2,1)}, bf16[8,576,512]{2,1,0:T(8,128)(2,1)}, bf16[8,576,512]{2...) while((s32[]{:T(128)}, bf16[8,64,4096]{2,1,0:T(8,128)(2,1)}, bf16[8,64,4096]{2,1,0:T(8,128)(2,1)}, ...), condition=%wide.region_7.8_spmd, body=%wide.region_2.7_spmd.sunk | while | flops 153714240 | bytes 17492984 | solution.py:121
  364.2 1.3 constant_dynamic-slice_fusion.3
  367.5 4.0 while.34
  372.9 1.3 constant_dynamic-slice_fusion.3
  376.2 4.0 while.34
  384.9 4.0 while.34
  393.6 4.0 while.34
  402.3 4.0 while.34
  411.0 4.0 while.34
  419.7 4.0 while.34
  428.4 4.0 while.34
  (246 shorter events, 71.4 us)
Async XLA Ops:
  0.0 0.8 copy-start
  3.1 10.3 %all-to-all-start = ((s32[16,1,12]{2,1,0:T(1,128)}), s32[16,1,12]{2,1,0:T(1,128)S(1)}, u32[]{:S(2)}, u32[]{:S(2)}) async-start(s32[16,1,12]{2,1,0:T(1,128)} %bitcast.8), calls=%async_computation | async-start | bytes 16384 | tf_op jit(solution)/shard_map/all_to_all | solution.py:99
  21.8 7.6 %copy-start.2 = (s32[384]{0:T(512)S(1)}, s32[384]{0:T(512)}, u32[]{:S(2)}) copy-start(s32[384]{0:T(512)} %param.17) | copy-start | bytes 4612
  21.8 279.8 %all-to-all-start.1 = ((bf16[16,12,2,32,512]{4,3,2,1,0:T(8,128)(2,1)}), bf16[16,12,2,32,512]{4,3,2,1,0:T(8,128)(2,1)}, u32[]{:S(2)}, u32[]{:S(2)}) async-start(bf16[16,12,2,32,512]{4,3,2,1,0:T(8,128)(2,1)} %bitcast.90), calls=%async_computation.1 | async-start | bytes 25165824 | tf_op jit(solution)/shard_map/all_to_all | solution.py:106
  348.0 7.3 %copy-start.3 = (bf16[8,64,512]{2,1,0:T(8,128)(2,1)S(1)}, bf16[8,64,512]{2,1,0:T(8,128)(2,1)}, u32[]{:S(2)}) copy-start(bf16[8,64,512]{2,1,0:T(8,128)(2,1)} %param.12) | copy-start | bytes 1572868
  348.0 7.3 %copy-start.4 = (bf16[8,64,512]{2,1,0:T(8,128)(2,1)S(1)}, bf16[8,64,512]{2,1,0:T(8,128)(2,1)}, u32[]{:S(2)}) copy-start(bf16[8,64,512]{2,1,0:T(8,128)(2,1)} %param.13) | copy-start | bytes 1572868
  433.9 0.7 copy-start.1
where the time goes:
time: 436 us; the launch traced here: 435 us
  waiting for transfers between devices  272 us (62%)
  local copies, waits for them, and re-layouts  80.3 us (18%)
  other arithmetic  42.2 us (10%)
  matrix products  24.5 us (6%)
  starting transfers between devices  14.1 us (3%)
    all_to_all x1, waiting for transfers between devices, local(): lax.all_to_all(outgoing, ('store', 'head'), split_axis=0, concat_axis=0,...  271 us
    dot_general x32, matrix products, one_head(): jnp.dot(weights, value_block, preferred_element_type=jnp.float32)  13.6 us
    gather x1, local copies, waits for them, and re-layouts, local(): incoming.reshape(peer_count * cap_dev, 2, PLEN, half_width)[slot_index]  11.1 us
    another operation x9, other arithmetic  11 us
    dot_general x32, matrix products, one_head(): jnp.dot(query_block, key_block.T, preferred_element_type=jnp.float32)  10.9 us
    while x32, local copies, waits for them, and re-layouts  10.6 us
    dynamic_slice x8, local copies, waits for them, and re-layouts, local(): return lax.map(one_request, (queries, key_rows, value_rows))  10.5 us
    convert_element_type x1, local copies, waits for them, and re-layouts, rerotate(): page_keys.astype(jnp.float32)  9.9 us
  transfers between devices with their start and end apart: 2, of which 2 were waited for; matrix products, arithmetic and copies ran while one was open for 1% of the time, Pallas kernels for 0%

commit v1 on v0

v1 whole, which is shorter than its diff:
```python
import functools

import jax
import jax.numpy as jnp
from jax import lax
from jax.experimental import pallas as pl
from jax.experimental.pallas import tpu as pltpu
from jax.sharding import PartitionSpec as P

HEAD_DIM = 128
NPASS = 16
PLEN = 32
CHUNKS = 2
ROWS_AT_ONCE = 256

rope_theta = 1000000.0
EXP2_SCALE = HEAD_DIM ** (-0.5) * 1.4426950408889634


def ranks_within(owner_ids):
    count = owner_ids.shape[0]
    same_owner = owner_ids[:, None] == owner_ids[None, :]
    earlier = jnp.arange(count)[None, :] < jnp.arange(count)[:, None]
    return jnp.sum(same_owner & earlier, axis=1)


def request_table(slot_index, local_row, total):
    hits = slot_index[:, None] == jnp.arange(total)[None, :]
    return jnp.sum(jnp.where(hits, local_row[:, None], 0), axis=0)


def pack_kernel(store_count, head_count, cap, width, wanted_ref, kv_ref, *rest):
    outs, sems = rest[:-1], rest[-1]
    half = kv_ref.shape[3] // head_count
    for chunk, out_ref in enumerate(outs):
        for head in range(head_count):
            lanes = pl.ds(head * half + chunk * width, width)

            def one_slot(i, carry):
                peer = (i // cap) * head_count + head
                j = i % cap
                row = wanted_ref[peer * cap + j]
                pltpu.make_async_copy(
                    kv_ref.at[row, :, :, lanes], out_ref.at[peer, j], sems.at[chunk]
                ).start()
                return carry

            lax.fori_loop(0, store_count * cap, one_slot, 0)
    for chunk, out_ref in enumerate(outs):
        pltpu.make_async_copy(out_ref, out_ref, sems.at[chunk]).wait()


def pack(wanted, passage_kv, store_count, head_count, cap, chunks):
    width = passage_kv.shape[3] // head_count // chunks
    shape = jax.ShapeDtypeStruct((store_count * head_count, cap, 2, PLEN, width), jnp.bfloat16)
    return pl.pallas_call(
        functools.partial(pack_kernel, store_count, head_count, cap, width),
        out_shape=[shape] * chunks,
        in_specs=[
            pl.BlockSpec(memory_space=pltpu.SMEM),
            pl.BlockSpec(memory_space=pltpu.VMEM),
        ],
        out_specs=[pl.BlockSpec(memory_space=pl.ANY)] * chunks,
        scratch_shapes=[pltpu.SemaphoreType.DMA((chunks,))],
        compiler_params=pltpu.CompilerParams(vmem_limit_bytes=16 * 1024 * 1024),
    )(wanted.reshape(-1), passage_kv)


def attend_kernel(group, slot_ref, q_ref, own_k_ref, own_v_ref, cos_ref, sin_ref, *rest):
    pages = rest[:NPASS]
    out_ref = rest[-1]
    qlen = q_ref.shape[1]
    kv_count = own_k_ref.shape[2] // HEAD_DIM
    span = ROWS_AT_ONCE // qlen
    ones = jnp.ones((NPASS * PLEN + qlen, HEAD_DIM), jnp.bfloat16)
    token = lax.broadcasted_iota(jnp.int32, (ROWS_AT_ONCE, qlen), 0) % qlen
    visible = lax.broadcasted_iota(jnp.int32, (ROWS_AT_ONCE, qlen), 1) <= token
    for kv in range(kv_count):
        lanes = slice(kv * HEAD_DIM, (kv + 1) * HEAD_DIM)
        keys = []
        for j in range(NPASS):
            stored = pages[j][0, 0, :, lanes].astype(jnp.float32)
            turned = stored * cos_ref[0, j : j + 1, :] + pltpu.roll(
                stored, HEAD_DIM // 2, 1
            ) * sin_ref[0, j : j + 1, :]
            keys.append(turned.astype(jnp.bfloat16))
        keys = jnp.concatenate(keys + [own_k_ref[0, :, lanes]], axis=0)
        values = jnp.concatenate(
            [pages[j][0, 1, :, lanes] for j in range(NPASS)] + [own_v_ref[0, :, lanes]], axis=0
        )
        values = jnp.concatenate([values, ones], axis=1)
        for first in range(0, group, span):
            heads = [kv * group + first + g for g in range(span)]
            question = jnp.concatenate(
                [q_ref[0, :, h * HEAD_DIM : (h + 1) * HEAD_DIM] for h in heads], axis=0
            )
            scores = lax.dot_general(
                question, keys, (((1,), (1,)), ((), ())), preferred_element_type=jnp.float32
            )
            own = jnp.where(visible, scores[:, NPASS * PLEN :], -jnp.inf)
            scores = jnp.concatenate([scores[:, : NPASS * PLEN], own], axis=1)
            peak = jnp.max(scores, axis=1, keepdims=True)
            expo = jnp.exp2((scores - peak) * EXP2_SCALE).astype(jnp.bfloat16)
            both = jnp.dot(expo, values, preferred_element_type=jnp.float32)
            result = (both[:, :HEAD_DIM] / both[:, HEAD_DIM:]).astype(jnp.bfloat16)
            for g, h in enumerate(heads):
                out_ref[0, :, h * HEAD_DIM : (h + 1) * HEAD_DIM] = result[g * qlen : (g + 1) * qlen]


def attend(chunk, chunks, slot_index, queries, own_keys, own_values, cosine, sine, fetched, so_far):
    requests, qlen, q_width = queries.shape
    kv_width = own_keys.shape[2] // chunks
    q_part = q_width // chunks
    group = q_part // kv_width
    page = fetched.shape[1:]

    def by_chunk(r, slots):
        return (r, 0, chunk)

    def by_request(r, slots):
        return (r, 0, 0)

    def page_spec(j):
        return pl.BlockSpec((1,) + page, lambda r, slots: (slots[r * NPASS + j], 0, 0, 0))

    in_specs = [
        pl.BlockSpec((1, qlen, q_part), by_chunk),
        pl.BlockSpec((1, qlen, kv_width), by_chunk),
        pl.BlockSpec((1, qlen, kv_width), by_chunk),
        pl.BlockSpec((1, NPASS, HEAD_DIM), by_request),
        pl.BlockSpec((1, NPASS, HEAD_DIM), by_request),
    ] + [page_spec(j) for j in range(NPASS)]
    operands = [queries, own_keys, own_values, cosine, sine] + [fetched] * NPASS
    aliases = {}
    if so_far is not None:
        in_specs.append(pl.BlockSpec(memory_space=pl.ANY))
        aliases = {1 + len(operands): 0}
        operands.append(so_far)
    keys = NPASS * PLEN + qlen
    return pl.pallas_call(
        functools.partial(attend_kernel, group),
        grid_spec=pltpu.PrefetchScalarGridSpec(
            num_scalar_prefetch=1,
            grid=(requests,),
            in_specs=in_specs,
            out_specs=pl.BlockSpec((1, qlen, q_part), by_chunk),
        ),
        out_shape=jax.ShapeDtypeStruct(queries.shape, jnp.bfloat16),
        input_output_aliases=aliases,
        compiler_params=pltpu.CompilerParams(vmem_limit_bytes=40 * 1024 * 1024),
        cost_estimate=pl.CostEstimate(
            flops=6 * requests * qlen * q_part * keys,
            bytes_accessed=4 * requests * qlen * q_part + 2 * requests * NPASS * 2 * PLEN * kv_width,
            transcendentals=requests * qlen * (q_part // HEAD_DIM) * keys,
        ),
    )(slot_index, *operands)


def local(queries, own_keys, own_values, passage_kv, passage_rows, retrieval, offsets):
    stored_count = passage_kv.shape[0]
    store_count = lax.axis_size("store")
    head_count = lax.axis_size("head")
    peer_count = store_count * head_count
    requests = queries.shape[0]
    pick_ids = retrieval.reshape(-1)
    pick_count = pick_ids.shape[0]
    cap_dev = 3 * pick_count // (2 * peer_count)
    store_rows = passage_rows[pick_ids]
    owner_dev = store_rows // stored_count
    local_row = store_rows % stored_count
    slot_index = owner_dev * cap_dev + ranks_within(owner_dev)
    asked = request_table(slot_index, local_row, peer_count * cap_dev).reshape(peer_count, cap_dev)
    wanted = lax.all_to_all(asked, ("store", "head"), split_axis=0, concat_axis=0, tiled=True)
    outgoing = pack(wanted, passage_kv, store_count, head_count, cap_dev, CHUNKS)

    turn_by = jnp.arange(pick_count, dtype=jnp.int32) % NPASS * PLEN - offsets[pick_ids]
    half_dim = HEAD_DIM // 2
    inverse_freq = rope_theta ** (-(jnp.arange(half_dim, dtype=jnp.float32) * 2.0) / HEAD_DIM)
    angles = turn_by.astype(jnp.float32)[:, None] * inverse_freq[None, :]
    cosine, sine = jnp.cos(angles), jnp.sin(angles)
    cosine = jnp.concatenate([cosine, cosine], axis=1).reshape(requests, NPASS, HEAD_DIM)
    sine = jnp.concatenate([-sine, sine], axis=1).reshape(requests, NPASS, HEAD_DIM)

    result = None
    for chunk in range(CHUNKS):
        incoming = lax.all_to_all(
            outgoing[chunk], ("store", "head"), split_axis=0, concat_axis=0, tiled=True
        )
        fetched = incoming.reshape((peer_count * cap_dev,) + incoming.shape[2:])
        result = attend(
            chunk, CHUNKS, slot_index, queries, own_keys, own_values, cosine, sine, fetched, result
        )
    return result


def solution(mesh):
    in_specs = (
        P(("parts", "store"), None, "head"),
        P(("parts", "store"), None, "head"),
        P(("parts", "store"), None, "head"),
        P(("parts", "store", "head"), None, None, None),
        P("parts"),
        P(("parts", "store"), None),
        P("parts"),
    )
    out_specs = P(("parts", "store"), None, "head")
    return jax.shard_map(local, mesh=mesh, in_specs=in_specs, out_specs=out_specs, check_vma=False)
```

time: 436 us -> 334 us (0.77)
  waiting for transfers between devices: 272 us -> 115 us
  blocking collectives: 0 us -> 153 us
  local copies, waits for them, and re-layouts: 80.3 us -> 13.1 us
  Pallas kernels: 0 us -> 45.2 us
  other arithmetic: 42.2 us -> 1.43 us
  matrix products: 24.5 us -> 0 us
  starting transfers between devices: 14.1 us -> 5.15 us
    all_to_all x2 -> x1, waiting for transfers between devices: 272 us -> 115 us  [local(): lax.all_to_all(outgoing[chunk], ('store', 'head'), split_axis=0, concat_a...]
    all_to_all x0 -> x2, blocking collectives: none -> 153 us  [the longest x1 143 us: local(): lax.all_to_all(outgoing[chunk], ('store', 'head'), split_axis=0, concat_a...]
    pallas_call x0 -> x3, Pallas kernels: none -> 45.2 us  [the longest x2 33.8 us: attend(): pl.pallas_call(functools.partial(attend_kernel, group), grid_spec=pltpu.P...]
    dot_general x64 -> x0, matrix products: 24.5 us -> none  [the longest x32 13.6 us: one_head(): jnp.dot(weights, value_block, preferred_element_type=jnp.float32)]
    gather x3 -> x2, local copies, waits for them, and re-layouts: 20.6 us -> 1.34 us  [local(): offsets[pick_ids]]
    convert_element_type x2 -> x0, local copies, waits for them, and re-layouts: 17.2 us -> none  [the longest x1 9.9 us: rerotate(): page_keys.astype(jnp.float32)]
    concatenate x3 -> x1, other arithmetic: 15.9 us -> 0.1 us  [local(): jnp.concatenate([cosine, cosine], axis=1).reshape(requests, NPASS, HEAD_DIM)]
    another operation x9 -> x0, other arithmetic: 11 us -> none
  transfers between devices with their start and end apart: 2 -> 1, of which waited for: 2 -> 1; matrix products, arithmetic and copies ran while one was open for 1% -> 1% of each run, Pallas kernels for 0% -> 5%
where the time goes in v1:
time: 334 us
  blocking collectives  153 us (46%)
  waiting for transfers between devices  115 us (34%)
  Pallas kernels  45.2 us (14%)
  local copies, waits for them, and re-layouts  13.1 us (4%)
  starting transfers between devices  5.15 us (2%)
    all_to_all x1, blocking collectives, local(): lax.all_to_all(outgoing[chunk], ('store', 'head'), split_axis=0, concat_a...  143 us
    all_to_all x1, waiting for transfers between devices, local(): lax.all_to_all(outgoing[chunk], ('store', 'head'), split_axis=0, concat_a...  115 us
    pallas_call x2, Pallas kernels, attend(): pl.pallas_call(functools.partial(attend_kernel, group), grid_spec=pltpu.P...  33.8 us
    pallas_call x1, Pallas kernels, pack(): pl.pallas_call(functools.partial(pack_kernel, store_count, head_count, ca...  11.4 us
    all_to_all x1, blocking collectives, local(): lax.all_to_all(asked, ('store', 'head'), split_axis=0, concat_axis=0, til...  10.2 us
    unnamed x18, local copies, waits for them, and re-layouts  9.06 us
  transfers between devices with their start and end apart: 1, of which 1 were waited for; matrix products, arithmetic and copies ran while one was open for 1% of the time, Pallas kernels for 5%

profile of v1, /device:TPU:15, one launch (start us, length us, event | category | flops | bytes accessed | tf_op | source)
XLA Modules:
  0.0 333.7 jit_solution(12372177454217521510)
XLA Ops:
  0.0 0.8 reshape.145
  0.8 1.3 gather_fusion
  2.1 0.2 convert_reduce_fusion
  2.3 0.1 select_reduce_fusion
  2.4 0.1 all_to_all.12
  2.5 10.2 %all_to_all.19 = s32[16,1,12]{2,1,0:T(1,128)S(1)} all-to-all(s32[16,1,12]{2,1,0:T(1,128)S(1)} %bitcast.21), channel_id=1, replica_groups=mesh['parts'=2,'store'=8,'head'=2] {'store','head'}, dimensions={0} | all-to-all | bytes 1536 | tf_op jit(solution)/shard_map/all_to_all | solution.py:173
  12.7 0.5 broadcast.181
  13.2 0.7 reduce.3
  13.8 0.1 reshape.146.wanted_ref
  13.9 0.0 copy-start.5
  13.9 1.9 copy-done.5
  15.8 11.4 %shard_map.73 = (bf16[16,12,2,32,256]{4,3,2,1,0:T(8,128)(2,1)S(1)}, bf16[16,12,2,32,256]{4,3,2,1,0:T(8,128)(2,1)S(1)}) custom-call(s32[192]{0:T(256)S(1)} %reshape.146.wanted_ref, bf16[24,2,32,1024]{3,2,1,0:T(8,128)(2,1)S(1)} %copy-done.5), custom_call_target="tpu_custom_call" | custom-call | tf_op jit(solution)/shard_map/pallas_call | solution.py:56
  27.3 143.3 %all_to_all.20 = bf16[16,12,2,32,256]{4,3,2,1,0:T(8,128)(2,1)} all-to-all(bf16[16,12,2,32,256]{4,3,2,1,0:T(8,128)(2,1)S(1)} %get-tuple-element.8), channel_id=1, replica_groups=mesh['parts'=2,'store'=8,'head'=2] {'store','head'}, dimensions={0} | all-to-all | bytes 12582912 | tf_op jit(solution)/shard_map/all_to_all | solution.py:186
  170.5 5.1 %all-to-all-start.1 = ((bf16[16,12,2,32,256]{4,3,2,1,0:T(8,128)(2,1)}), bf16[16,12,2,32,256]{4,3,2,1,0:T(8,128)(2,1)}, u32[]{:S(2)}, u32[]{:S(2)}) async-start(bf16[16,12,2,32,256]{4,3,2,1,0:T(8,128)(2,1)} %copy-done.4), calls=%async_computation.1 | async-start | bytes 12582912 | tf_op jit(solution)/shard_map/all_to_all | solution.py:186
  175.7 1.3 gather_fusion.1
  177.0 0.1 gather.10
  177.1 0.3 fusion.1
  177.4 0.1 pad_maximum_fusion
  177.5 2.8 copy-done.1
  180.3 2.2 copy-done.2
  182.5 15.4 %shard_map.74.rest_16_ = bf16[8,64,4096]{2,1,0:T(8,128)(2,1)} custom-call(s32[128]{0:T(128)S(1)} %multiply_add_fusion.slot_ref, bf16[8,64,4096]{2,1,0:T(8,128)(2,1)S(1)} %copy-done.2, bf16[8,64,512]{2,1,0:T(8,128)(2,1)S(1)} %copy-done.6, bf16[8,64,512]{2,1,0:T(8,128)(2,1)S(1)} %copy-done.7, f32[8,16,128]{2,1,0:T(8,128)S(1)} %get-tuple-element.14.cos_ref, ...), custom_call_target="tpu_custom_call" | custom-call | flops 3623878656 | bytes 8388608 | tf_op jit(solution)/shard_map/pallas_call | solution.py:140
  197.9 115.2 %all-to-all-done.1 = bf16[16,12,2,32,256]{4,3,2,1,0:T(8,128)(2,1)} async-done(((bf16[16,12,2,32,256]{4,3,2,1,0:T(8,128)(2,1)}), bf16[16,12,2,32,256]{4,3,2,1,0:T(8,128)(2,1)}, u32[]{:S(2)}, u32[]{:S(2)}) %all-to-all-start.1) | async-done | bytes 6291488 | tf_op jit(solution)/shard_map/all_to_all | solution.py:186
  313.1 2.2 copy-done.3
  315.3 18.4 %shard_map.75 = bf16[8,64,4096]{2,1,0:T(8,128)(2,1)} custom-call(s32[128]{0:T(128)S(1)} %multiply_add_fusion.slot_ref, bf16[8,64,4096]{2,1,0:T(8,128)(2,1)S(1)} %copy-done.3, bf16[8,64,512]{2,1,0:T(8,128)(2,1)S(1)} %copy-done.6, bf16[8,64,512]{2,1,0:T(8,128)(2,1)S(1)} %copy-done.7, ...), custom_call_target="tpu_custom_call", output_to_operand_aliasing={{}: (22, {})} | custom-call | flops 3623878656 | bytes 8388608 | tf_op jit(solution)/shard_map/pallas_call | solution.py:140
  (19 shorter events, 0.1 us)
Async XLA Ops:
  0.0 0.8 copy-start
  13.9 1.9 copy-start.5
  27.2 143.3 %copy-start.4 = (bf16[16,12,2,32,256]{4,3,2,1,0:T(8,128)(2,1)}, bf16[16,12,2,32,256]{4,3,2,1,0:T(8,128)(2,1)S(1)}, u32[]{:S(2)}) copy-start(bf16[16,12,2,32,256]{4,3,2,1,0:T(8,128)(2,1)S(1)} %get-tuple-element.7) | copy-start | bytes 18874372
  170.5 5.2 %copy-start.8 = (s32[384]{0:T(512)S(1)}, s32[384]{0:T(512)}, u32[]{:S(2)}) copy-start(s32[384]{0:T(512)} %param.13) | copy-start | bytes 4612
  170.5 7.0 %copy-start.6 = (bf16[8,64,512]{2,1,0:T(8,128)(2,1)S(1)}, bf16[8,64,512]{2,1,0:T(8,128)(2,1)}, u32[]{:S(2)}) copy-start(bf16[8,64,512]{2,1,0:T(8,128)(2,1)} %own_k_ref.3) | copy-start | bytes 1572868
  170.5 7.0 %copy-start.7 = (bf16[8,64,512]{2,1,0:T(8,128)(2,1)S(1)}, bf16[8,64,512]{2,1,0:T(8,128)(2,1)}, u32[]{:S(2)}) copy-start(bf16[8,64,512]{2,1,0:T(8,128)(2,1)} %own_v_ref.3) | copy-start | bytes 1572868
  170.5 142.6 %all-to-all-start.1 = ((bf16[16,12,2,32,256]{4,3,2,1,0:T(8,128)(2,1)}), bf16[16,12,2,32,256]{4,3,2,1,0:T(8,128)(2,1)}, u32[]{:S(2)}, u32[]{:S(2)}) async-start(bf16[16,12,2,32,256]{4,3,2,1,0:T(8,128)(2,1)} %copy-done.4), calls=%async_computation.1 | async-start | bytes 12582912 | tf_op jit(solution)/shard_map/all_to_all | solution.py:186
  177.5 2.8 copy-start.1
  180.3 2.2 copy-start.2
  313.1 2.2 copy-start.3

commit v2 on v1

--- a/solution.py
+++ b/solution.py
@@ -10,7 +10,8 @@
 HEAD_DIM = 128
 NPASS = 16
 PLEN = 32
-CHUNKS = 2
+CHUNKS = 1
+PLANE = 4
 ROWS_AT_ONCE = 256
 
 rope_theta = 1000000.0
@@ -156,6 +157,188 @@
     )(slot_index, *operands)
 
 
+def here():
+    store, head = lax.axis_index("store"), lax.axis_index("head")
+    return store * 2 + head, (store * 2 + head) // PLANE, (store * 2 + head) % PLANE
+
+
+def remote(src, dst, send_sem, recv_sem, peer):
+    return pltpu.make_async_remote_copy(
+        src_ref=src,
+        dst_ref=dst,
+        send_sem=send_sem,
+        recv_sem=recv_sem,
+        device_id={"store": peer // 2, "head": peer % 2},
+        device_id_type=pl.DeviceIdType.MESH,
+    )
+
+
+def greet_all(me, count):
+    barrier = pltpu.get_barrier_semaphore()
+
+    def greet(k, carry):
+        peer = (me + k) % count
+        pl.semaphore_signal(
+            barrier,
+            inc=1,
+            device_id={"store": peer // 2, "head": peer % 2},
+            device_id_type=pl.DeviceIdType.MESH,
+        )
+        return carry
+
+    lax.fori_loop(1, count, greet, 0)
+    pl.semaphore_wait(barrier, count - 1)
+
+
+def near_kernel(out_ref, kv_ref, in_ref, relay_ref, send, recv, keep):
+    me, plane, spot = here()
+    outer = (plane == 0) | (plane == 3)
+    inner = (plane == 1) | (plane == 2)
+    greet_all(me, 4 * PLANE)
+    whole = remote(
+        kv_ref, relay_ref, send.at[8], recv.at[8], jnp.where(plane == 0, 2, 1) * PLANE + spot
+    )
+
+    def block(k, target_plane):
+        peer = target_plane * PLANE + (spot + k % PLANE) % PLANE
+        return remote(out_ref.at[peer], in_ref.at[me], send.at[k], recv.at[k], peer)
+
+    out_plane = jnp.where(plane == 1, 0, 3)
+
+    @pl.when(outer)
+    def _():
+        whole.start()
+
+    @pl.when(inner)
+    def _():
+        for k in range(PLANE):
+            block(PLANE + k, out_plane).start()
+
+    for k in range(1, PLANE):
+        block(k, plane).start()
+    own = pltpu.make_async_copy(out_ref.at[me], in_ref.at[me], keep)
+    own.start()
+    own.wait()
+    for k in range(1, PLANE):
+        block(k, plane).wait()
+
+    @pl.when(outer)
+    def _():
+        for k in range(PLANE):
+            block(PLANE + k, plane).wait_recv()
+        whole.wait_send()
+
+    @pl.when(inner)
+    def _():
+        for k in range(PLANE):
+            block(PLANE + k, out_plane).wait_send()
+        whole.wait_recv()
+
+
+def far_kernel(out_ref, relay_ref, have_ref, in_ref, send, recv, keep):
+    me, plane, spot = here()
+    outer = (plane == 0) | (plane == 3)
+    inner = (plane == 1) | (plane == 2)
+    greet_all(me, 4 * PLANE)
+    origin = jnp.where(plane == 2, 0, 3) * PLANE + spot
+
+    def block(k, target_plane):
+        peer = target_plane * PLANE + (spot + k % PLANE) % PLANE
+        return remote(out_ref.at[peer], in_ref.at[me], send.at[k], recv.at[k], peer)
+
+    def relayed(k, step, target_plane):
+        spot_there = (spot + k % PLANE) % PLANE
+        return remote(
+            relay_ref.at[step, spot_there],
+            in_ref.at[origin],
+            send.at[k],
+            recv.at[k],
+            target_plane * PLANE + spot_there,
+        )
+
+    inward = jnp.where(plane == 0, 1, 2)
+    across = jnp.where(plane == 1, 2, 1)
+    beyond = jnp.where(plane == 1, 3, 0)
+    out_plane = jnp.where(plane == 1, 0, 3)
+    own = pltpu.make_async_copy(relay_ref.at[0, spot], in_ref.at[origin], keep)
+
+    @pl.when(outer)
+    def _():
+        for k in range(PLANE):
+            block(k, inward).start()
+        for k in range(PLANE):
+            block(k, inward).wait_send()
+        for k in range(PLANE):
+            block(2 * PLANE + k, inward).wait_recv()
+            relayed(4 * PLANE + k, 1, inward).wait_recv()
+
+    @pl.when(inner)
+    def _():
+        for k in range(PLANE):
+            block(2 * PLANE + k, beyond).start()
+            relayed(4 * PLANE + k, 1, out_plane).start()
+            block(PLANE + k, across).start()
+        for k in range(1, PLANE):
+            relayed(3 * PLANE + k, 0, plane).start()
+        own.start()
+        own.wait()
+        for k in range(PLANE):
+            block(2 * PLANE + k, beyond).wait_send()
+            relayed(4 * PLANE + k, 1, out_plane).wait_send()
+            block(PLANE + k, across).wait()
+            block(k, across).wait_recv()
+        for k in range(1, PLANE):
+            relayed(3 * PLANE + k, 0, plane).wait()
+
+
+def exchange(wanted_all, outgoing, passage_kv):
+    any_space = pl.BlockSpec(memory_space=pl.ANY)
+    incoming, relay = pl.pallas_call(
+        near_kernel,
+        out_shape=[
+            jax.ShapeDtypeStruct(outgoing.shape, jnp.bfloat16),
+            jax.ShapeDtypeStruct(passage_kv.shape, jnp.bfloat16),
+        ],
+        in_specs=[any_space] * 2,
+        out_specs=[any_space] * 2,
+        scratch_shapes=[
+            pltpu.SemaphoreType.DMA((9,)),
+            pltpu.SemaphoreType.DMA((9,)),
+            pltpu.SemaphoreType.DMA,
+        ],
+        compiler_params=pltpu.CompilerParams(collective_id=1, has_side_effects=True),
+    )(outgoing, passage_kv)
+    me, plane, spot = here()
+    origin = jnp.where(plane == 2, 0, 3) * PLANE + spot
+    for_origin = lax.dynamic_index_in_dim(wanted_all, origin, 1, keepdims=False)
+    cap = for_origin.shape[1]
+    by_plane = for_origin.reshape(4, 2, cap)
+    out_plane = jnp.where(plane == 1, 0, 3)
+    lists = jnp.concatenate(
+        [
+            lax.dynamic_index_in_dim(by_plane, plane, 0, keepdims=False),
+            lax.dynamic_index_in_dim(by_plane, out_plane, 0, keepdims=False),
+        ],
+        axis=0,
+    )
+    lists = jnp.repeat(lists, 2, axis=0)
+    relay_out = pack(lists, relay, 4, 2, cap, 1)[0]
+    relay_out = relay_out.reshape((2, PLANE) + relay_out.shape[1:])
+    return pl.pallas_call(
+        far_kernel,
+        out_shape=jax.ShapeDtypeStruct(outgoing.shape, jnp.bfloat16),
+        in_specs=[any_space] * 3,
+        out_specs=any_space,
+        input_output_aliases={2: 0},
+        scratch_shapes=[
+            pltpu.SemaphoreType.DMA((5 * PLANE,)),
+            pltpu.SemaphoreType.DMA((5 * PLANE,)),
+            pltpu.SemaphoreType.DMA,
+        ],
+        compiler_params=pltpu.CompilerParams(collective_id=2, has_side_effects=True),
+    )(outgoing, relay_out, incoming)
+
+
 def local(queries, own_keys, own_values, passage_kv, passage_rows, retrieval, offsets):
     stored_count = passage_kv.shape[0]
     store_count = lax.axis_size("store")
@@ -170,7 +353,14 @@
     local_row = store_rows % stored_count
     slot_index = owner_dev * cap_dev + ranks_within(owner_dev)
     asked = request_table(slot_index, local_row, peer_count * cap_dev).reshape(peer_count, cap_dev)
-    wanted = lax.all_to_all(asked, ("store", "head"), split_axis=0, concat_axis=0, tiled=True)
+    relays = store_count == 8 and head_count == 2 and 2 * cap_dev >= stored_count
+    if relays:
+        told = jnp.broadcast_to(asked[None], (peer_count,) + asked.shape)
+        told = lax.all_to_all(told, ("store", "head"), split_axis=0, concat_axis=0, tiled=True)
+        wanted_all = told.reshape(store_count, head_count, peer_count, cap_dev)[:, 0]
+        wanted = jnp.repeat(wanted_all[:, here()[0]], head_count, axis=0)
+    else:
+        wanted = lax.all_to_all(asked, ("store", "head"), split_axis=0, concat_axis=0, tiled=True)
     outgoing = pack(wanted, passage_kv, store_count, head_count, cap_dev, CHUNKS)
 
     turn_by = jnp.arange(pick_count, dtype=jnp.int32) % NPASS * PLEN - offsets[pick_ids]
@@ -183,9 +373,12 @@
 
     result = None
     for chunk in range(CHUNKS):
-        incoming = lax.all_to_all(
-            outgoing[chunk], ("store", "head"), split_axis=0, concat_axis=0, tiled=True
-        )
+        if relays:
+            incoming = exchange(wanted_all, outgoing[chunk], passage_kv)
+        else:
+            incoming = lax.all_to_all(
+                outgoing[chunk], ("store", "head"), split_axis=0, concat_axis=0, tiled=True
+            )
         fetched = incoming.reshape((peer_count * cap_dev,) + incoming.shape[2:])
         result = attend(
             chunk, CHUNKS, slot_index, queries, own_keys, own_values, cosine, sine, fetched, result

time: 334 us -> 283 us (0.85)
  Pallas kernels: 45.2 us -> 252 us
  blocking collectives: 153 us -> 0 us
  waiting for transfers between devices: 115 us -> 1.88 us
  local copies, waits for them, and re-layouts: 13.1 us -> 19.3 us
    pallas_call x0 -> x2, Pallas kernels: none -> 213 us  [the longest x1 140 us: exchange(): pl.pallas_call(far_kernel, out_shape=jax.ShapeDtypeStruct(outgoing.shape,...]
    all_to_all x2 -> x0, blocking collectives: 153 us -> none  [the longest x1 143 us: local(): lax.all_to_all(outgoing[chunk], ('store', 'head'), split_axis=0, concat_a...]
    all_to_all x1, waiting for transfers between devices: 115 us -> 1.88 us  [local(): lax.all_to_all(told, ('store', 'head'), split_axis=0, concat_axis=0, tile...]
    pallas_call x2 -> x1, Pallas kernels: 33.8 us -> 28.1 us  [attend(): pl.pallas_call(functools.partial(attend_kernel, group), grid_spec=pltpu.P...]
    unnamed x18 -> x19, local copies, waits for them, and re-layouts: 9.06 us -> 14 us
    pallas_call x1 -> x2, Pallas kernels: 11.4 us -> 10.7 us  [pack(): pl.pallas_call(functools.partial(pack_kernel, store_count, head_count, ca...]
  transfers between devices with their start and end apart: 1 -> 1, of which waited for: 1 -> 1; matrix products, arithmetic and copies ran while one was open for 1% -> 1% of each run, Pallas kernels for 5% -> 0%
where the time goes in v2:
time: 283 us; the launch traced here: 281 us
  Pallas kernels  252 us (89%)
  local copies, waits for them, and re-layouts  19.3 us (7%)
  starting transfers between devices  6.55 us (2%)
    pallas_call x1, Pallas kernels, exchange(): pl.pallas_call(far_kernel, out_shape=jax.ShapeDtypeStruct(outgoing.shape,...  140 us
    pallas_call x1, Pallas kernels, exchange(): pl.pallas_call(near_kernel, out_shape=[jax.ShapeDtypeStruct(outgoing.shap...  73.2 us
    pallas_call x1, Pallas kernels, attend(): pl.pallas_call(functools.partial(attend_kernel, group), grid_spec=pltpu.P...  28.1 us
    unnamed x19, local copies, waits for them, and re-layouts  14 us
    pallas_call x2, Pallas kernels, pack(): pl.pallas_call(functools.partial(pack_kernel, store_count, head_count, ca...  10.7 us
    all_to_all x1, starting transfers between devices, local(): lax.all_to_all(told, ('store', 'head'), split_axis=0, concat_axis=0, tile...  6.55 us
  transfers between devices with their start and end apart: 1, of which 1 were waited for; matrix products, arithmetic and copies ran while one was open for 1% of the time, Pallas kernels for 0%

profile of v2, /device:TPU:15, one launch (start us, length us, event | category | flops | bytes accessed | tf_op | source)
XLA Modules:
  0.0 281.3 jit_solution(7514282251269975561)
XLA Ops:
  0.0 0.8 reshape.149
  0.8 1.3 gather_fusion
  2.1 0.2 convert_reduce_fusion
  2.3 0.1 select_reduce_fusion
  2.6 0.7 reshape.170
  3.3 6.6 %all-to-all-start = ((s32[16,1,192]{2,1,0:T(1,128)}), s32[16,1,192]{2,1,0:T(1,128)S(1)}, u32[]{:S(2)}, u32[]{:S(2)}) async-start(s32[16,1,192]{2,1,0:T(1,128)} %reshape.170), calls=%async_computation | async-start | bytes 32768 | tf_op jit(solution)/shard_map/all_to_all | solution.py:359
  9.9 1.6 gather_fusion.1
  11.6 0.3 fusion.1
  12.1 1.9 all-to-all-done
  14.0 0.5 broadcast.184
  14.5 0.7 reduce
  15.4 0.3 constant_dynamic-slice_fusion
  15.7 0.1 copy.20
  15.9 1.9 copy-done.3
  17.8 7.0 %shard_map.73.out_ref = bf16[16,12,2,32,512]{4,3,2,1,0:T(8,128)(2,1)S(1)} custom-call(s32[192]{0:T(256)S(1)} %reshape_reshape.6.wanted_ref, bf16[24,2,32,1024]{3,2,1,0:T(8,128)(2,1)S(1)} %copy-done.3), custom_call_target="tpu_custom_call" | custom-call | tf_op jit(solution)/shard_map/pallas_call | solution.py:57
  24.8 4.5 %copy-done.1 = bf16[16,12,2,32,512]{4,3,2,1,0:T(8,128)(2,1)} copy-done((bf16[16,12,2,32,512]{4,3,2,1,0:T(8,128)(2,1)}, bf16[16,12,2,32,512]{4,3,2,1,0:T(8,128)(2,1)S(1)}, u32[]{:S(2)}) %copy-start.1) | copy-done | bytes 12582936
  29.3 73.2 %shard_map.74 = (bf16[16,12,2,32,512]{4,3,2,1,0:T(8,128)(2,1)}, bf16[24,2,32,1024]{3,2,1,0:T(8,128)(2,1)}) custom-call(bf16[16,12,2,32,512]{4,3,2,1,0:T(8,128)(2,1)} %copy-done.1, bf16[24,2,32,1024]{3,2,1,0:T(8,128)(2,1)} %kv_ref.3), custom_call_target="tpu_custom_call" | custom-call | tf_op jit(solution)/shard_map/pallas_call | solution.py:296
  102.5 0.1 copy.21
  102.8 1.9 copy-done.5
  104.7 3.8 %shard_map.75 = bf16[8,12,2,32,512]{4,3,2,1,0:T(8,128)(2,1)S(1)} custom-call(s32[96]{0:T(128)S(1)} %reshape_reshape.7.wanted_ref, bf16[24,2,32,1024]{3,2,1,0:T(8,128)(2,1)S(1)} %copy-done.5), custom_call_target="tpu_custom_call" | custom-call | tf_op jit(solution)/shard_map/pallas_call | solution.py:57
  108.5 2.7 copy-done.2
  111.1 139.8 %shard_map.76 = bf16[16,12,2,32,512]{4,3,2,1,0:T(8,128)(2,1)} custom-call(bf16[16,12,2,32,512]{4,3,2,1,0:T(8,128)(2,1)} %copy-done.1, bf16[2,4,12,2,32,512]{5,4,3,2,1,0:T(8,128)(2,1)} %bitcast.14, bf16[16,12,2,32,512]{4,3,2,1,0:T(8,128)(2,1)} %get-tuple-element.8.have_ref), custom_call_target="tpu_custom_call", output_to_operand_aliasing={{}: (2, {})} | custom-call | tf_op jit(solution)/shard_map/pallas_call | solution.py:327
  251.0 2.2 copy-done.4
  253.2 28.1 %shard_map.77 = bf16[8,64,4096]{2,1,0:T(8,128)(2,1)} custom-call(s32[128]{0:T(128)S(1)} %multiply_add_fusion.slot_ref, bf16[8,64,4096]{2,1,0:T(8,128)(2,1)S(1)} %copy-done.4, bf16[8,64,512]{2,1,0:T(8,128)(2,1)S(1)} %copy-done.6, bf16[8,64,512]{2,1,0:T(8,128)(2,1)S(1)} %copy-done.7, f32[8,16,128]{2,1,0:T(8,128)S(1)} %get-tuple-element.18.cos_ref, ...), custom_call_target="tpu_custom_call" | custom-call | flops 7247757312 | bytes 16777216 | tf_op jit(solution)/shard_map/pallas_call | solution.py:141
  (31 shorter events, 0.8 us)
Async XLA Ops:
  0.0 0.8 copy-start
  3.3 10.7 %all-to-all-start = ((s32[16,1,192]{2,1,0:T(1,128)}), s32[16,1,192]{2,1,0:T(1,128)S(1)}, u32[]{:S(2)}, u32[]{:S(2)}) async-start(s32[16,1,192]{2,1,0:T(1,128)} %reshape.170), calls=%async_computation | async-start | bytes 32768 | tf_op jit(solution)/shard_map/all_to_all | solution.py:359
  15.9 1.9 copy-start.3
  24.8 4.5 %copy-start.1 = (bf16[16,12,2,32,512]{4,3,2,1,0:T(8,128)(2,1)}, bf16[16,12,2,32,512]{4,3,2,1,0:T(8,128)(2,1)S(1)}, u32[]{:S(2)}) copy-start(bf16[16,12,2,32,512]{4,3,2,1,0:T(8,128)(2,1)S(1)} %shard_map.73.out_ref) | copy-start | bytes 37748740
  102.8 1.9 copy-start.5
  108.4 2.7 copy-start.2
  111.1 139.8 %copy-start.6 = (bf16[8,64,512]{2,1,0:T(8,128)(2,1)S(1)}, bf16[8,64,512]{2,1,0:T(8,128)(2,1)}, u32[]{:S(2)}) copy-start(bf16[8,64,512]{2,1,0:T(8,128)(2,1)} %own_k_ref.1) | copy-start | bytes 1572868
  111.1 139.8 %copy-start.7 = (bf16[8,64,512]{2,1,0:T(8,128)(2,1)S(1)}, bf16[8,64,512]{2,1,0:T(8,128)(2,1)}, u32[]{:S(2)}) copy-start(bf16[8,64,512]{2,1,0:T(8,128)(2,1)} %own_v_ref.1) | copy-start | bytes 1572868
  251.0 2.2 copy-start.4

commit v3 on v2

--- a/solution.py
+++ b/solution.py
@@ -12,6 +12,7 @@
 PLEN = 32
 CHUNKS = 1
 PLANE = 4
+VMEM_LIMIT = 60 * 1024 * 1024
 ROWS_AT_ONCE = 256
 
 rope_theta = 1000000.0
@@ -63,7 +64,7 @@
         ],
         out_specs=[pl.BlockSpec(memory_space=pl.ANY)] * chunks,
         scratch_shapes=[pltpu.SemaphoreType.DMA((chunks,))],
-        compiler_params=pltpu.CompilerParams(vmem_limit_bytes=16 * 1024 * 1024),
+        compiler_params=pltpu.CompilerParams(vmem_limit_bytes=VMEM_LIMIT),
     )(wanted.reshape(-1), passage_kv)
 
 
@@ -148,7 +149,7 @@
         ),
         out_shape=jax.ShapeDtypeStruct(queries.shape, jnp.bfloat16),
         input_output_aliases=aliases,
-        compiler_params=pltpu.CompilerParams(vmem_limit_bytes=40 * 1024 * 1024),
+        compiler_params=pltpu.CompilerParams(vmem_limit_bytes=VMEM_LIMIT),
         cost_estimate=pl.CostEstimate(
             flops=6 * requests * qlen * q_part * keys,
             bytes_accessed=4 * requests * qlen * q_part + 2 * requests * NPASS * 2 * PLEN * kv_width,
@@ -190,24 +191,16 @@
     pl.semaphore_wait(barrier, count - 1)
 
 
-def near_kernel(out_ref, kv_ref, in_ref, relay_ref, send, recv, keep):
+def near_kernel(out_ref, in_ref, send, recv, keep):
     me, plane, spot = here()
     outer = (plane == 0) | (plane == 3)
     inner = (plane == 1) | (plane == 2)
     greet_all(me, 4 * PLANE)
-    whole = remote(
-        kv_ref, relay_ref, send.at[8], recv.at[8], jnp.where(plane == 0, 2, 1) * PLANE + spot
-    )
-
     def block(k, target_plane):
         peer = target_plane * PLANE + (spot + k % PLANE) % PLANE
         return remote(out_ref.at[peer], in_ref.at[me], send.at[k], recv.at[k], peer)
 
     out_plane = jnp.where(plane == 1, 0, 3)
-
-    @pl.when(outer)
-    def _():
-        whole.start()
 
     @pl.when(inner)
     def _():
@@ -226,13 +219,11 @@
     def _():
         for k in range(PLANE):
             block(PLANE + k, plane).wait_recv()
-        whole.wait_send()
 
     @pl.when(inner)
     def _():
         for k in range(PLANE):
             block(PLANE + k, out_plane).wait_send()
-        whole.wait_recv()
 
 
 def far_kernel(out_ref, relay_ref, have_ref, in_ref, send, recv, keep):
@@ -291,23 +282,20 @@
             relayed(3 * PLANE + k, 0, plane).wait()
 
 
-def exchange(wanted_all, outgoing, passage_kv):
+def exchange(wanted_all, outgoing, relay):
     any_space = pl.BlockSpec(memory_space=pl.ANY)
-    incoming, relay = pl.pallas_call(
+    incoming = pl.pallas_call(
         near_kernel,
-        out_shape=[
-            jax.ShapeDtypeStruct(outgoing.shape, jnp.bfloat16),
-            jax.ShapeDtypeStruct(passage_kv.shape, jnp.bfloat16),
-        ],
-        in_specs=[any_space] * 2,
-        out_specs=[any_space] * 2,
+        out_shape=jax.ShapeDtypeStruct(outgoing.shape, jnp.bfloat16),
+        in_specs=[any_space],
+        out_specs=any_space,
         scratch_shapes=[
-            pltpu.SemaphoreType.DMA((9,)),
-            pltpu.SemaphoreType.DMA((9,)),
+            pltpu.SemaphoreType.DMA((2 * PLANE,)),
+            pltpu.SemaphoreType.DMA((2 * PLANE,)),
             pltpu.SemaphoreType.DMA,
         ],
-        compiler_params=pltpu.CompilerParams(collective_id=1, has_side_effects=True),
-    )(outgoing, passage_kv)
+        compiler_params=pltpu.CompilerParams(collective_id=1, has_side_effects=True, vmem_limit_bytes=VMEM_LIMIT),
+    )(outgoing)
     me, plane, spot = here()
     origin = jnp.where(plane == 2, 0, 3) * PLANE + spot
     for_origin = lax.dynamic_index_in_dim(wanted_all, origin, 1, keepdims=False)
@@ -335,7 +323,7 @@
             pltpu.SemaphoreType.DMA((5 * PLANE,)),
             pltpu.SemaphoreType.DMA,
         ],
-        compiler_params=pltpu.CompilerParams(collective_id=2, has_side_effects=True),
+        compiler_params=pltpu.CompilerParams(collective_id=2, has_side_effects=True, vmem_limit_bytes=VMEM_LIMIT),
     )(outgoing, relay_out, incoming)
 
 
@@ -355,6 +343,9 @@
     asked = request_table(slot_index, local_row, peer_count * cap_dev).reshape(peer_count, cap_dev)
     relays = store_count == 8 and head_count == 2 and 2 * cap_dev >= stored_count
     if relays:
+        hops = [(spot, 2 * PLANE + spot) for spot in range(PLANE)]
+        hops += [(3 * PLANE + spot, PLANE + spot) for spot in range(PLANE)]
+        relay = lax.ppermute(passage_kv, ("store", "head"), hops)
         told = jnp.broadcast_to(asked[None], (peer_count,) + asked.shape)
         told = lax.all_to_all(told, ("store", "head"), split_axis=0, concat_axis=0, tiled=True)
         wanted_all = told.reshape(store_count, head_count, peer_count, cap_dev)[:, 0]
@@ -374,7 +365,7 @@
     result = None
     for chunk in range(CHUNKS):
         if relays:
-            incoming = exchange(wanted_all, outgoing[chunk], passage_kv)
+            incoming = exchange(wanted_all, outgoing[chunk], relay)
         else:
             incoming = lax.all_to_all(
                 outgoing[chunk], ("store", "head"), split_axis=0, concat_axis=0, tiled=True

time: 283 us -> 333 us (1.18)
  waiting for transfers between devices: 1.88 us -> 58.3 us
  local copies, waits for them, and re-layouts: 19.3 us -> 8.9 us
    all_to_all x1, waiting for transfers between devices: 1.88 us -> 58.3 us  [local(): lax.all_to_all(told, ('store', 'head'), split_axis=0, concat_axis=0, tile...]
    unnamed x19 -> x9, local copies, waits for them, and re-layouts: 14 us -> 2.5 us
  transfers between devices with their start and end apart: 1 -> 2, of which waited for: 1 -> 1; matrix products, arithmetic and copies ran while one was open for 1% -> 3% of each run, Pallas kernels for 0% -> 24%
where the time goes in v3:
time: 333 us; the launch traced here: 331 us
  Pallas kernels  252 us (76%)
  waiting for transfers between devices  58.3 us (18%)
  starting transfers between devices  9.12 us (3%)
  local copies, waits for them, and re-layouts  8.9 us (3%)
    pallas_call x1, Pallas kernels, exchange(): pl.pallas_call(far_kernel, out_shape=jax.ShapeDtypeStruct(outgoing.shape,...  141 us
    pallas_call x1, Pallas kernels, exchange(): pl.pallas_call(near_kernel, out_shape=jax.ShapeDtypeStruct(outgoing.shape...  71.6 us
    all_to_all x1, waiting for transfers between devices, local(): lax.all_to_all(told, ('store', 'head'), split_axis=0, concat_axis=0, tile...  58.3 us
    pallas_call x1, Pallas kernels, attend(): pl.pallas_call(functools.partial(attend_kernel, group), grid_spec=pltpu.P...  28.5 us
    pallas_call x2, Pallas kernels, pack(): pl.pallas_call(functools.partial(pack_kernel, store_count, head_count, ca...  11 us
    all_to_all x1, starting transfers between devices, local(): lax.all_to_all(told, ('store', 'head'), split_axis=0, concat_axis=0, tile...  7.71 us
  transfers between devices with their start and end apart: 2, of which 1 were waited for; matrix products, arithmetic and copies ran while one was open for 3% of the time, Pallas kernels for 24%

profile of v3, /device:TPU:15, one launch (start us, length us, event | category | flops | bytes accessed | tf_op | source)
XLA Modules:
  0.0 331.0 jit_solution(6823417552883388820)
XLA Ops:
  0.0 1.4 collective-permute-start
  1.4 0.8 reshape.149
  2.2 1.3 gather_fusion
  3.5 0.2 convert_reduce_fusion
  3.7 0.1 select_reduce_fusion
  4.0 0.7 reshape.170
  4.7 7.7 %all-to-all-start = ((s32[16,1,192]{2,1,0:T(1,128)}), s32[16,1,192]{2,1,0:T(1,128)S(1)}, u32[]{:S(2)}, u32[]{:S(2)}) async-start(s32[16,1,192]{2,1,0:T(1,128)} %reshape.170), calls=%async_computation | async-start | bytes 32768 | tf_op jit(solution)/shard_map/all_to_all | solution.py:350
  12.4 1.6 gather_fusion.1
  14.2 0.3 fusion.1
  14.5 0.8 pad_maximum_fusion
  15.3 58.3 %all-to-all-done = s32[16,1,192]{2,1,0:T(1,128)S(1)} async-done(((s32[16,1,192]{2,1,0:T(1,128)}), s32[16,1,192]{2,1,0:T(1,128)S(1)}, u32[]{:S(2)}, u32[]{:S(2)}) %all-to-all-start) | async-done | bytes 12320 | tf_op jit(solution)/shard_map/all_to_all | solution.py:350
  73.5 0.5 broadcast.184
  74.1 0.7 reduce
  74.9 0.3 constant_dynamic-slice_fusion
  75.2 0.1 copy.20
  75.3 0.7 reshape_reshape.6.wanted_ref
  76.0 6.5 %shard_map.73.out_ref = bf16[16,12,2,32,512]{4,3,2,1,0:T(8,128)(2,1)} custom-call(s32[192]{0:T(256)} %reshape_reshape.6.wanted_ref, bf16[24,2,32,1024]{3,2,1,0:T(8,128)(2,1)} %kv_ref.1), custom_call_target="tpu_custom_call" | custom-call | tf_op jit(solution)/shard_map/pallas_call | solution.py:58
  82.6 71.6 %shard_map.75.have_ref = bf16[16,12,2,32,512]{4,3,2,1,0:T(8,128)(2,1)} custom-call(bf16[16,12,2,32,512]{4,3,2,1,0:T(8,128)(2,1)} %shard_map.73.out_ref), custom_call_target="tpu_custom_call" | custom-call | tf_op jit(solution)/shard_map/pallas_call | solution.py:287
  154.1 0.1 copy.21
  154.3 0.7 reshape_reshape.7.wanted_ref
  155.0 1.7 copy-done.1
  156.6 4.5 %shard_map.74 = bf16[8,12,2,32,512]{4,3,2,1,0:T(8,128)(2,1)} custom-call(s32[96]{0:T(128)} %reshape_reshape.7.wanted_ref, bf16[24,2,32,1024]{3,2,1,0:T(8,128)(2,1)} %copy-done.1), custom_call_target="tpu_custom_call" | custom-call | tf_op jit(solution)/shard_map/pallas_call | solution.py:58
  161.2 141.4 %shard_map.76 = bf16[16,12,2,32,512]{4,3,2,1,0:T(8,128)(2,1)} custom-call(bf16[16,12,2,32,512]{4,3,2,1,0:T(8,128)(2,1)} %shard_map.73.out_ref, bf16[2,4,12,2,32,512]{5,4,3,2,1,0:T(8,128)(2,1)} %bitcast.30, bf16[16,12,2,32,512]{4,3,2,1,0:T(8,128)(2,1)} %shard_map.75.have_ref), custom_call_target="tpu_custom_call", output_to_operand_aliasing={{}: (2, {})} | custom-call | tf_op jit(solution)/shard_map/pallas_call | solution.py:315
  302.6 28.5 %shard_map.77 = bf16[8,64,4096]{2,1,0:T(8,128)(2,1)} custom-call(s32[128]{0:T(128)} %copy-done.2, bf16[8,64,4096]{2,1,0:T(8,128)(2,1)} %q_ref.1, bf16[8,64,512]{2,1,0:T(8,128)(2,1)} %own_k_ref.1, bf16[8,64,512]{2,1,0:T(8,128)(2,1)} %own_v_ref.1, f32[8,16,128]{2,1,0:T(8,128)} %get-tuple-element.14.cos_ref, f32[8,16,128]{2,1,0:T(8,128)} %get-tuple-element.15.sin_ref, ...), custom_call_target="tpu_custom_call" | custom-call | flops 7247757312 | bytes 16777216 | tf_op jit(solution)/shard_map/pallas_call | solution.py:142
  (23 shorter events, 0.5 us)
Async XLA Ops:
  0.0 2.2 copy-start
  0.0 155.0 %collective-permute-start = (bf16[24,2,32,1024]{3,2,1,0:T(8,128)(2,1)}, bf16[24,2,32,1024]{3,2,1,0:T(8,128)(2,1)S(1)}, u32[]{:S(2)}, u32[]{:S(2)}) collective-permute-start(bf16[24,2,32,1024]{3,2,1,0:T(8,128)(2,1)} %kv_ref.1), channel_id=1, source_target_pairs={{0,8},{1,9},{2,10},{3,11},{12,4},{13,5},{14,6},{15,7},{16,24},{17,... | collective-permute-start | bytes 9437192 | tf_op jit(solution)/shard_map/ppermute | solution.py:348
  3.7 78.8 %copy-start.2 = (s32[128]{0:T(128)}, s32[128]{0:T(128)S(1)}, u32[]{:S(2)}) copy-start(s32[128]{0:T(128)S(1)} %multiply_add_fusion.slot_ref) | copy-start | bytes 1540
  4.7 68.8 %all-to-all-start = ((s32[16,1,192]{2,1,0:T(1,128)}), s32[16,1,192]{2,1,0:T(1,128)S(1)}, u32[]{:S(2)}, u32[]{:S(2)}) async-start(s32[16,1,192]{2,1,0:T(1,128)} %reshape.170), calls=%async_computation | async-start | bytes 32768 | tf_op jit(solution)/shard_map/all_to_all | solution.py:350
  155.0 1.7 copy-start.1

commit v4 on v2

--- a/solution.py
+++ b/solution.py
@@ -12,6 +12,7 @@
 PLEN = 32
 CHUNKS = 1
 PLANE = 4
+VMEM_LIMIT = 60 * 1024 * 1024
 ROWS_AT_ONCE = 256
 
 rope_theta = 1000000.0
@@ -63,7 +64,7 @@
         ],
         out_specs=[pl.BlockSpec(memory_space=pl.ANY)] * chunks,
         scratch_shapes=[pltpu.SemaphoreType.DMA((chunks,))],
-        compiler_params=pltpu.CompilerParams(vmem_limit_bytes=16 * 1024 * 1024),
+        compiler_params=pltpu.CompilerParams(vmem_limit_bytes=VMEM_LIMIT),
     )(wanted.reshape(-1), passage_kv)
 
 
@@ -148,7 +149,7 @@
         ),
         out_shape=jax.ShapeDtypeStruct(queries.shape, jnp.bfloat16),
         input_output_aliases=aliases,
-        compiler_params=pltpu.CompilerParams(vmem_limit_bytes=40 * 1024 * 1024),
+        compiler_params=pltpu.CompilerParams(vmem_limit_bytes=VMEM_LIMIT),
         cost_estimate=pl.CostEstimate(
             flops=6 * requests * qlen * q_part * keys,
             bytes_accessed=4 * requests * qlen * q_part + 2 * requests * NPASS * 2 * PLEN * kv_width,
@@ -289,6 +290,48 @@
             block(k, across).wait_recv()
         for k in range(1, PLANE):
             relayed(3 * PLANE + k, 0, plane).wait()
+
+
+def tell_kernel(asked_ref, told_ref, send, recv):
+    me, plane, spot = here()
+    count = told_ref.shape[0]
+    store, head = me // 2, me % 2
+    barrier = pltpu.get_barrier_semaphore()
+
+    def greet(k, carry):
+        pl.semaphore_signal(
+            barrier,
+            inc=1,
+            device_id={"store": (store + k) % count},
+            device_id_type=pl.DeviceIdType.MESH,
+        )
+        return carry
+
+    lax.fori_loop(1, count, greet, 0)
+    told_ref[store] = asked_ref[...]
+    pl.semaphore_wait(barrier, count - 1)
+
+    def table(k):
+        peer = (store + k) % count * 2 + head
+        return remote(asked_ref, told_ref.at[store], send.at[k], recv.at[k], peer)
+
+    for k in range(1, count):
+        table(k).start()
+    for k in range(1, count):
+        table(k).wait()
+
+
+def tell(asked, store_count):
+    table = jnp.pad(asked, ((0, 0), (0, 128 - asked.shape[1])))
+    told = pl.pallas_call(
+        tell_kernel,
+        out_shape=jax.ShapeDtypeStruct((store_count,) + table.shape, jnp.int32),
+        in_specs=[pl.BlockSpec(memory_space=pltpu.VMEM)],
+        out_specs=pl.BlockSpec(memory_space=pltpu.VMEM),
+        scratch_shapes=[pltpu.SemaphoreType.DMA((store_count,))] * 2,
+        compiler_params=pltpu.CompilerParams(collective_id=3, has_side_effects=True),
+    )(table)
+    return told[:, :, : asked.shape[1]]
 
 
 def exchange(wanted_all, outgoing, passage_kv):
@@ -306,7 +349,7 @@
             pltpu.SemaphoreType.DMA((9,)),
             pltpu.SemaphoreType.DMA,
         ],
-        compiler_params=pltpu.CompilerParams(collective_id=1, has_side_effects=True),
+        compiler_params=pltpu.CompilerParams(collective_id=1, has_side_effects=True, vmem_limit_bytes=VMEM_LIMIT),
     )(outgoing, passage_kv)
     me, plane, spot = here()
     origin = jnp.where(plane == 2, 0, 3) * PLANE + spot
@@ -335,7 +378,7 @@
             pltpu.SemaphoreType.DMA((5 * PLANE,)),
             pltpu.SemaphoreType.DMA,
         ],
-        compiler_params=pltpu.CompilerParams(collective_id=2, has_side_effects=True),
+        compiler_params=pltpu.CompilerParams(collective_id=2, has_side_effects=True, vmem_limit_bytes=VMEM_LIMIT),
     )(outgoing, relay_out, incoming)
 
 
@@ -355,9 +398,7 @@
     asked = request_table(slot_index, local_row, peer_count * cap_dev).reshape(peer_count, cap_dev)
     relays = store_count == 8 and head_count == 2 and 2 * cap_dev >= stored_count
     if relays:
-        told = jnp.broadcast_to(asked[None], (peer_count,) + asked.shape)
-        told = lax.all_to_all(told, ("store", "head"), split_axis=0, concat_axis=0, tiled=True)
-        wanted_all = told.reshape(store_count, head_count, peer_count, cap_dev)[:, 0]
+        wanted_all = tell(asked, store_count)
         wanted = jnp.repeat(wanted_all[:, here()[0]], head_count, axis=0)
     else:
         wanted = lax.all_to_all(asked, ("store", "head"), split_axis=0, concat_axis=0, tiled=True)

time: 283 us -> 271 us (0.958)
  local copies, waits for them, and re-layouts: 19.3 us -> 6.16 us
  Pallas kernels: 252 us -> 261 us
  starting transfers between devices: 6.55 us -> 0 us
    unnamed x19 -> x6, local copies, waits for them, and re-layouts: 14 us -> 0.01 us
    pallas_call x0 -> x1, Pallas kernels: none -> 7.27 us  [tell(): pl.pallas_call(tell_kernel, out_shape=jax.ShapeDtypeStruct((store_count,)...]
    all_to_all x1 -> x0, starting transfers between devices: 6.55 us -> none  [local(): lax.all_to_all(told, ('store', 'head'), split_axis=0, concat_axis=0, tile...]
  transfers between devices with their start and end apart: 1 -> 0, of which waited for: 1 -> 0; matrix products, arithmetic and copies ran while one was open for 1% -> 0% of each run, Pallas kernels for 0% -> 0%
where the time goes in v4:
time: 271 us; the launch traced here: 269 us
  Pallas kernels  261 us (96%)
  local copies, waits for them, and re-layouts  6.16 us (2%)
    pallas_call x1, Pallas kernels, exchange(): pl.pallas_call(far_kernel, out_shape=jax.ShapeDtypeStruct(outgoing.shape,...  141 us
    pallas_call x1, Pallas kernels, exchange(): pl.pallas_call(near_kernel, out_shape=[jax.ShapeDtypeStruct(outgoing.shap...  73.2 us
    pallas_call x1, Pallas kernels, attend(): pl.pallas_call(functools.partial(attend_kernel, group), grid_spec=pltpu.P...  28.4 us
    pallas_call x2, Pallas kernels, pack(): pl.pallas_call(functools.partial(pack_kernel, store_count, head_count, ca...  11 us
    pallas_call x1, Pallas kernels, tell(): pl.pallas_call(tell_kernel, out_shape=jax.ShapeDtypeStruct((store_count,)...  7.27 us

profile of v4, /device:TPU:15, one launch (start us, length us, event | category | flops | bytes accessed | tf_op | source)
XLA Modules:
  0.0 268.8 jit_solution(7490610041925358276)
XLA Ops:
  0.0 0.0 copy-start
  0.0 0.8 reshape.144
  0.8 0.0 copy-done
  0.8 1.3 gather_fusion
  2.1 0.2 convert_reduce_fusion
  2.3 0.0 copy-start.2
  2.3 0.1 select_reduce_fusion
  2.4 0.1 reshape.145
  2.5 0.6 pad.4.asked_ref
  3.1 7.3 %shard_map.73 = s32[8,16,128]{2,1,0:T(8,128)} custom-call(s32[16,128]{1,0:T(8,128)} %pad.4.asked_ref), custom_call_target="tpu_custom_call" | custom-call | tf_op jit(solution)/shard_map/pallas_call | solution.py:326
  10.4 0.8 constant_dynamic-slice_fusion
  11.2 0.7 reshape_reshape.6.wanted_ref
  11.9 6.5 %shard_map.74.out_ref = bf16[16,12,2,32,512]{4,3,2,1,0:T(8,128)(2,1)} custom-call(s32[192]{0:T(256)} %reshape_reshape.6.wanted_ref, bf16[24,2,32,1024]{3,2,1,0:T(8,128)(2,1)} %kv_ref.3), custom_call_target="tpu_custom_call" | custom-call | tf_op jit(solution)/shard_map/pallas_call | solution.py:58
  18.4 0.0 copy-done.2
  18.4 73.2 %shard_map.75 = (bf16[16,12,2,32,512]{4,3,2,1,0:T(8,128)(2,1)}, bf16[24,2,32,1024]{3,2,1,0:T(8,128)(2,1)}) custom-call(bf16[16,12,2,32,512]{4,3,2,1,0:T(8,128)(2,1)} %shard_map.74.out_ref, bf16[24,2,32,1024]{3,2,1,0:T(8,128)(2,1)} %kv_ref.3), custom_call_target="tpu_custom_call" | custom-call | tf_op jit(solution)/shard_map/pallas_call | solution.py:339
  91.6 0.6 reshape_reshape.7.wanted_ref
  92.2 4.5 %shard_map.76 = bf16[8,12,2,32,512]{4,3,2,1,0:T(8,128)(2,1)} custom-call(s32[96]{0:T(128)} %reshape_reshape.7.wanted_ref, bf16[24,2,32,1024]{3,2,1,0:T(8,128)(2,1)} %get-tuple-element.7.kv_ref), custom_call_target="tpu_custom_call" | custom-call | tf_op jit(solution)/shard_map/pallas_call | solution.py:58
  96.7 0.0 copy-start.1
  96.7 141.1 %shard_map.77 = bf16[16,12,2,32,512]{4,3,2,1,0:T(8,128)(2,1)} custom-call(bf16[16,12,2,32,512]{4,3,2,1,0:T(8,128)(2,1)} %shard_map.74.out_ref, bf16[2,4,12,2,32,512]{5,4,3,2,1,0:T(8,128)(2,1)} %bitcast.27, bf16[16,12,2,32,512]{4,3,2,1,0:T(8,128)(2,1)} %get-tuple-element.8.have_ref), custom_call_target="tpu_custom_call", output_to_operand_aliasing={{}: (2, {})} | custom-call | tf_op jit(solution)/shard_map/pallas_call | solution.py:370
  237.9 1.3 gather_fusion.1
  239.1 0.1 gather.10
  239.3 0.3 fusion.1
  239.6 0.8 pad_maximum_fusion
  240.3 28.4 %shard_map.78 = bf16[8,64,4096]{2,1,0:T(8,128)(2,1)} custom-call(s32[128]{0:T(128)} %copy-done.2, bf16[8,64,4096]{2,1,0:T(8,128)(2,1)} %q_ref.1, bf16[8,64,512]{2,1,0:T(8,128)(2,1)} %own_k_ref.1, bf16[8,64,512]{2,1,0:T(8,128)(2,1)} %own_v_ref.1, f32[8,16,128]{2,1,0:T(8,128)} %get-tuple-element.18.cos_ref, f32[8,16,128]{2,1,0:T(8,128)} %get-tuple-element.19.sin_ref, ...), custom_call_target="tpu_custom_call" | custom-call | flops 7247757312 | bytes 16777216 | tf_op jit(solution)/shard_map/pallas_call | solution.py:142
  (11 shorter events, 0.1 us)
Async XLA Ops:
  0.0 0.8 copy-start
  2.3 16.1 %copy-start.2 = (s32[128]{0:T(128)}, s32[128]{0:T(128)S(1)}, u32[]{:S(2)}) copy-start(s32[128]{0:T(128)S(1)} %multiply_add_fusion.slot_ref) | copy-start | bytes 1540
  96.7 141.1 %copy-start.1 = (s32[384]{0:T(512)S(1)}, s32[384]{0:T(512)}, u32[]{:S(2)}) copy-start(s32[384]{0:T(512)} %param.13) | copy-start | bytes 4612

commit v5 on v4

--- a/solution.py
+++ b/solution.py
@@ -13,7 +13,7 @@
 CHUNKS = 1
 PLANE = 4
 VMEM_LIMIT = 60 * 1024 * 1024
-ROWS_AT_ONCE = 256
+ROWS_AT_ONCE = 128
 
 rope_theta = 1000000.0
 EXP2_SCALE = HEAD_DIM ** (-0.5) * 1.4426950408889634
@@ -191,105 +191,114 @@
     pl.semaphore_wait(barrier, count - 1)
 
 
-def near_kernel(out_ref, kv_ref, in_ref, relay_ref, send, recv, keep):
+def exchange_kernel(lists_ref, out_ref, kv_ref, in_ref, store_buf, relay_buf, send, recv, keep):
     me, plane, spot = here()
     outer = (plane == 0) | (plane == 3)
     inner = (plane == 1) | (plane == 2)
     greet_all(me, 4 * PLANE)
-    whole = remote(
-        kv_ref, relay_ref, send.at[8], recv.at[8], jnp.where(plane == 0, 2, 1) * PLANE + spot
-    )
-
-    def block(k, target_plane):
-        peer = target_plane * PLANE + (spot + k % PLANE) % PLANE
-        return remote(out_ref.at[peer], in_ref.at[me], send.at[k], recv.at[k], peer)
-
-    out_plane = jnp.where(plane == 1, 0, 3)
-
-    @pl.when(outer)
-    def _():
-        whole.start()
-
-    @pl.when(inner)
-    def _():
-        for k in range(PLANE):
-            block(PLANE + k, out_plane).start()
-
-    for k in range(1, PLANE):
-        block(k, plane).start()
-    own = pltpu.make_async_copy(out_ref.at[me], in_ref.at[me], keep)
-    own.start()
-    own.wait()
-    for k in range(1, PLANE):
-        block(k, plane).wait()
-
-    @pl.when(outer)
-    def _():
-        for k in range(PLANE):
-            block(PLANE + k, plane).wait_recv()
-        whole.wait_send()
-
-    @pl.when(inner)
-    def _():
-        for k in range(PLANE):
-            block(PLANE + k, out_plane).wait_send()
-        whole.wait_recv()
-
-
-def far_kernel(out_ref, relay_ref, have_ref, in_ref, send, recv, keep):
-    me, plane, spot = here()
-    outer = (plane == 0) | (plane == 3)
-    inner = (plane == 1) | (plane == 2)
-    greet_all(me, 4 * PLANE)
-    origin = jnp.where(plane == 2, 0, 3) * PLANE + spot
-
-    def block(k, target_plane):
-        peer = target_plane * PLANE + (spot + k % PLANE) % PLANE
-        return remote(out_ref.at[peer], in_ref.at[me], send.at[k], recv.at[k], peer)
-
-    def relayed(k, step, target_plane):
-        spot_there = (spot + k % PLANE) % PLANE
-        return remote(
-            relay_ref.at[step, spot_there],
-            in_ref.at[origin],
-            send.at[k],
-            recv.at[k],
-            target_plane * PLANE + spot_there,
-        )
-
     inward = jnp.where(plane == 0, 1, 2)
     across = jnp.where(plane == 1, 2, 1)
     beyond = jnp.where(plane == 1, 3, 0)
     out_plane = jnp.where(plane == 1, 0, 3)
-    own = pltpu.make_async_copy(relay_ref.at[0, spot], in_ref.at[origin], keep)
+    origin = jnp.where(plane == 2, 0, 3) * PLANE + spot
+    cap = relay_buf.shape[2]
+    half = relay_buf.shape[5]
+    OWN, OUT, INWARD, ACROSS, BEYOND, RELAY_OWN, RELAY_OUT = range(0, 7 * PLANE, PLANE)
+    whole_sem = 7 * PLANE
+    whole = remote(
+        kv_ref,
+        store_buf,
+        send.at[whole_sem],
+        recv.at[whole_sem],
+        jnp.where(plane == 0, 2, 1) * PLANE + spot,
+    )
+
+    def block(kind, k, target_plane):
+        peer = target_plane * PLANE + (spot + k) % PLANE
+        return remote(out_ref.at[peer], in_ref.at[me], send.at[kind + k], recv.at[kind + k], peer)
+
+    def relayed(kind, k, step, target_plane):
+        spot_there = (spot + k) % PLANE
+        return remote(
+            relay_buf.at[step, spot_there],
+            in_ref.at[origin],
+            send.at[kind + k],
+            recv.at[kind + k],
+            target_plane * PLANE + spot_there,
+        )
+
+    def fill(step, k):
+        spot_there = (spot + k) % PLANE
+        head = spot_there % 2
+
+        for side in range(2):
+
+            @pl.when(head == side)
+            def _():
+                def one_page(i, carry):
+                    row = lists_ref[(step * PLANE + spot_there) * cap + i]
+                    relay_buf[step, spot_there, i] = store_buf[
+                        row, :, :, side * half : (side + 1) * half
+                    ]
+                    return carry
+
+                lax.fori_loop(0, cap, one_page, 0)
+
+    own = pltpu.make_async_copy(out_ref.at[me], in_ref.at[me], keep.at[0])
+    own_relay = pltpu.make_async_copy(relay_buf.at[0, spot], in_ref.at[origin], keep.at[1])
 
     @pl.when(outer)
     def _():
-        for k in range(PLANE):
-            block(k, inward).start()
-        for k in range(PLANE):
-            block(k, inward).wait_send()
-        for k in range(PLANE):
-            block(2 * PLANE + k, inward).wait_recv()
-            relayed(4 * PLANE + k, 1, inward).wait_recv()
+        whole.start()
 
     @pl.when(inner)
     def _():
         for k in range(PLANE):
-            block(2 * PLANE + k, beyond).start()
-            relayed(4 * PLANE + k, 1, out_plane).start()
-            block(PLANE + k, across).start()
+            block(BEYOND, k, beyond).start()
+            block(OUT, k, out_plane).start()
+
+    for k in range(1, PLANE):
+        block(OWN, k, plane).start()
+    own.start()
+
+    @pl.when(outer)
+    def _():
+        whole.wait_send()
+        for k in range(PLANE):
+            block(INWARD, k, inward).start()
+        for k in range(PLANE):
+            block(INWARD, k, inward).wait_send()
+        for k in range(PLANE):
+            block(OUT, k, plane).wait_recv()
+            block(BEYOND, k, plane).wait_recv()
+            relayed(RELAY_OUT, k, 1, plane).wait_recv()
+
+    @pl.when(inner)
+    def _():
+        whole.wait_recv()
+        for k in range(PLANE):
+            block(ACROSS, k, across).start()
+        for k in range(PLANE):
+            fill(1, k)
+            relayed(RELAY_OUT, k, 1, out_plane).start()
         for k in range(1, PLANE):
-            relayed(3 * PLANE + k, 0, plane).start()
-        own.start()
-        own.wait()
-        for k in range(PLANE):
-            block(2 * PLANE + k, beyond).wait_send()
-            relayed(4 * PLANE + k, 1, out_plane).wait_send()
-            block(PLANE + k, across).wait()
-            block(k, across).wait_recv()
+            fill(0, k)
+            relayed(RELAY_OWN, k, 0, plane).start()
+        fill(0, 0)
+        own_relay.start()
+        own_relay.wait()
+        for k in range(PLANE):
+            block(BEYOND, k, beyond).wait_send()
+            block(OUT, k, out_plane).wait_send()
+            relayed(RELAY_OUT, k, 1, out_plane).wait_send()
+            block(ACROSS, k, across).wait()
+            block(INWARD, k, plane).wait_recv()
         for k in range(1, PLANE):
-            relayed(3 * PLANE + k, 0, plane).wait()
+            relayed(RELAY_OWN, k, 0, plane).wait()
+
+    own.wait()
+    for k in range(1, PLANE):
+        block(OWN, k, plane).wait()
 
 
 def tell_kernel(asked_ref, told_ref, send, recv):
@@ -336,21 +345,6 @@
 
 def exchange(wanted_all, outgoing, passage_kv):
     any_space = pl.BlockSpec(memory_space=pl.ANY)
-    incoming, relay = pl.pallas_call(
-        near_kernel,
-        out_shape=[
-            jax.ShapeDtypeStruct(outgoing.shape, jnp.bfloat16),
-            jax.ShapeDtypeStruct(passage_kv.shape, jnp.bfloat16),
-        ],
-        in_specs=[any_space] * 2,
-        out_specs=[any_space] * 2,
-        scratch_shapes=[
-            pltpu.SemaphoreType.DMA((9,)),
-            pltpu.SemaphoreType.DMA((9,)),
-            pltpu.SemaphoreType.DMA,
-        ],
-        compiler_params=pltpu.CompilerParams(collective_id=1, has_side_effects=True, vmem_limit_bytes=VMEM_LIMIT),
-    )(outgoing, passage_kv)
     me, plane, spot = here()
     origin = jnp.where(plane == 2, 0, 3) * PLANE + spot
     for_origin = lax.dynamic_index_in_dim(wanted_all, origin, 1, keepdims=False)
@@ -364,22 +358,23 @@
         ],
         axis=0,
     )
-    lists = jnp.repeat(lists, 2, axis=0)
-    relay_out = pack(lists, relay, 4, 2, cap, 1)[0]
-    relay_out = relay_out.reshape((2, PLANE) + relay_out.shape[1:])
+    lists = jnp.repeat(lists, 2, axis=0).reshape(-1)
     return pl.pallas_call(
-        far_kernel,
+        exchange_kernel,
         out_shape=jax.ShapeDtypeStruct(outgoing.shape, jnp.bfloat16),
-        in_specs=[any_space] * 3,
+        in_specs=[pl.BlockSpec(memory_space=pltpu.SMEM), any_space, any_space],
         out_specs=any_space,
-        input_output_aliases={2: 0},
         scratch_shapes=[
-            pltpu.SemaphoreType.DMA((5 * PLANE,)),
-            pltpu.SemaphoreType.DMA((5 * PLANE,)),
-            pltpu.SemaphoreType.DMA,
+            pltpu.VMEM(passage_kv.shape, jnp.bfloat16),
+            pltpu.VMEM((2, PLANE) + outgoing.shape[1:], jnp.bfloat16),
+            pltpu.SemaphoreType.DMA((7 * PLANE + 1,)),
+            pltpu.SemaphoreType.DMA((7 * PLANE + 1,)),
+            pltpu.SemaphoreType.DMA((2,)),
         ],
-        compiler_params=pltpu.CompilerParams(collective_id=2, has_side_effects=True, vmem_limit_bytes=VMEM_LIMIT),
-    )(outgoing, relay_out, incoming)
+        compiler_params=pltpu.CompilerParams(
+            collective_id=1, has_side_effects=True, vmem_limit_bytes=VMEM_LIMIT
+        ),
+    )(lists, outgoing, passage_kv)
 
 
 def local(queries, own_keys, own_values, passage_kv, passage_rows, retrieval, offsets):

time: 271 us -> 260 us (0.959)
  Pallas kernels: 261 us -> 250 us
    pallas_call x2 -> x1, Pallas kernels: 11 us -> 6.48 us  [pack(): pl.pallas_call(functools.partial(pack_kernel, store_count, head_count, ca...]
    pallas_call x2 -> x1, Pallas kernels: 214 us -> 210 us  [exchange(): pl.pallas_call(exchange_kernel, out_shape=jax.ShapeDtypeStruct(outgoing.s...]
    pallas_call x1, Pallas kernels: 28.4 us -> 25.6 us  [attend(): pl.pallas_call(functools.partial(attend_kernel, group), grid_spec=pltpu.P...]
where the time goes in v5:
time: 260 us; the launch traced here: 257 us
  Pallas kernels  250 us (96%)
  local copies, waits for them, and re-layouts  6.16 us (2%)
    pallas_call x1, Pallas kernels, exchange(): pl.pallas_call(exchange_kernel, out_shape=jax.ShapeDtypeStruct(outgoing.s...  210 us
    pallas_call x1, Pallas kernels, attend(): pl.pallas_call(functools.partial(attend_kernel, group), grid_spec=pltpu.P...  25.6 us
    pallas_call x1, Pallas kernels, tell(): pl.pallas_call(tell_kernel, out_shape=jax.ShapeDtypeStruct((store_count,)...  7.27 us
    pallas_call x1, Pallas kernels, pack(): pl.pallas_call(functools.partial(pack_kernel, store_count, head_count, ca...  6.48 us

profile of v5, /device:TPU:15, one launch (start us, length us, event | category | flops | bytes accessed | tf_op | source)
XLA Modules:
  0.0 257.3 jit_solution(5027294314178208334)
XLA Ops:
  0.0 0.0 copy-start
  0.0 0.8 reshape.141
  0.8 0.0 copy-done
  0.8 1.3 gather_fusion
  2.1 0.2 convert_reduce_fusion
  2.3 0.0 copy-start.2
  2.3 0.1 select_reduce_fusion
  2.4 0.1 reshape.142
  2.5 0.6 pad.4.asked_ref
  3.1 7.3 %shard_map.73 = s32[8,16,128]{2,1,0:T(8,128)} custom-call(s32[16,128]{1,0:T(8,128)} %pad.4.asked_ref), custom_call_target="tpu_custom_call" | custom-call | tf_op jit(solution)/shard_map/pallas_call | solution.py:335
  10.4 0.8 constant_dynamic-slice_fusion
  11.2 0.7 reshape_reshape.7.wanted_ref
  11.9 6.5 %shard_map.74.out_ref = bf16[16,12,2,32,512]{4,3,2,1,0:T(8,128)(2,1)} custom-call(s32[192]{0:T(256)} %reshape_reshape.7.wanted_ref, bf16[24,2,32,1024]{3,2,1,0:T(8,128)(2,1)} %kv_ref.3), custom_call_target="tpu_custom_call" | custom-call | tf_op jit(solution)/shard_map/pallas_call | solution.py:58
  18.3 0.0 copy-done.2
  18.4 0.6 reshape_reshape.6.lists_ref
  19.0 0.0 copy-start.1
  19.0 210.3 %shard_map.75 = bf16[16,12,2,32,512]{4,3,2,1,0:T(8,128)(2,1)} custom-call(s32[96]{0:T(128)} %reshape_reshape.6.lists_ref, bf16[16,12,2,32,512]{4,3,2,1,0:T(8,128)(2,1)} %shard_map.74.out_ref, bf16[24,2,32,1024]{3,2,1,0:T(8,128)(2,1)} %kv_ref.3), custom_call_target="tpu_custom_call" | custom-call | tf_op jit(solution)/shard_map/pallas_call | solution.py:362
  229.3 0.0 copy-done.1
  229.3 1.3 gather_fusion.1
  230.6 0.1 gather.10
  230.7 0.3 fusion.1
  231.0 0.8 pad_maximum_fusion
  231.8 25.6 %shard_map.76 = bf16[8,64,4096]{2,1,0:T(8,128)(2,1)} custom-call(s32[128]{0:T(128)} %copy-done.2, bf16[8,64,4096]{2,1,0:T(8,128)(2,1)} %q_ref.1, bf16[8,64,512]{2,1,0:T(8,128)(2,1)} %own_k_ref.1, bf16[8,64,512]{2,1,0:T(8,128)(2,1)} %own_v_ref.1, f32[8,16,128]{2,1,0:T(8,128)} %get-tuple-element.14.cos_ref, f32[8,16,128]{2,1,0:T(8,128)} %get-tuple-element.15.sin_ref, ...), custom_call_target="tpu_custom_call" | custom-call | flops 7247757312 | bytes 16777216 | tf_op jit(solution)/shard_map/pallas_call | solution.py:142
  (10 shorter events, 0.1 us)
Async XLA Ops:
  0.0 0.8 copy-start
  2.3 16.1 %copy-start.2 = (s32[128]{0:T(128)}, s32[128]{0:T(128)S(1)}, u32[]{:S(2)}) copy-start(s32[128]{0:T(128)S(1)} %multiply_add_fusion.slot_ref) | copy-start | bytes 1540
  19.0 210.3 %copy-start.1 = (s32[384]{0:T(512)S(1)}, s32[384]{0:T(512)}, u32[]{:S(2)}) copy-start(s32[384]{0:T(512)} %param.13) | copy-start | bytes 4612

commit v6 on v5

--- a/solution.py
+++ b/solution.py
@@ -191,8 +191,12 @@
     pl.semaphore_wait(barrier, count - 1)
 
 
-def exchange_kernel(lists_ref, out_ref, kv_ref, in_ref, store_buf, relay_buf, send, recv, keep):
+def exchange_kernel(
+    lists_ref, kv_ref, in_ref, mine_buf, out_ref, store_buf, relay_buf, send, recv, keep
+):
     me, plane, spot = here()
+    mine = pltpu.make_async_copy(kv_ref, mine_buf, keep.at[2])
+    mine.start()
     outer = (plane == 0) | (plane == 3)
     inner = (plane == 1) | (plane == 2)
     greet_all(me, 4 * PLANE)
@@ -227,22 +231,26 @@
             target_plane * PLANE + spot_there,
         )
 
-    def fill(step, k):
-        spot_there = (spot + k) % PLANE
-        head = spot_there % 2
-
+    def fill(source, target, first, head):
         for side in range(2):
 
             @pl.when(head == side)
             def _():
                 def one_page(i, carry):
-                    row = lists_ref[(step * PLANE + spot_there) * cap + i]
-                    relay_buf[step, spot_there, i] = store_buf[
-                        row, :, :, side * half : (side + 1) * half
-                    ]
+                    row = lists_ref[first + i]
+                    target[i] = source[row, :, :, side * half : (side + 1) * half]
                     return carry
 
                 lax.fori_loop(0, cap, one_page, 0)
+
+    def fill_own(k, target_plane):
+        peer = target_plane * PLANE + (spot + k) % PLANE
+        fill(mine_buf, out_ref.at[peer], peer * cap, peer % 2)
+
+    def fill_relay(step, k):
+        spot_there = (spot + k) % PLANE
+        first = (4 * PLANE + step * PLANE + spot_there) * cap
+        fill(store_buf, relay_buf.at[step, spot_there], first, spot_there % 2)
 
     own = pltpu.make_async_copy(out_ref.at[me], in_ref.at[me], keep.at[0])
     own_relay = pltpu.make_async_copy(relay_buf.at[0, spot], in_ref.at[origin], keep.at[1])
@@ -251,18 +259,26 @@
     def _():
         whole.start()
 
+    mine.wait()
+
     @pl.when(inner)
     def _():
         for k in range(PLANE):
+            fill_own(k, out_plane)
+            block(OUT, k, out_plane).start()
+            fill_own(k, beyond)
             block(BEYOND, k, beyond).start()
-            block(OUT, k, out_plane).start()
 
     for k in range(1, PLANE):
+        fill_own(k, plane)
         block(OWN, k, plane).start()
+    fill_own(0, plane)
     own.start()
 
     @pl.when(outer)
     def _():
+        for k in range(PLANE):
+            fill_own(k, inward)
         whole.wait_send()
         for k in range(PLANE):
             block(INWARD, k, inward).start()
@@ -275,16 +291,18 @@
 
     @pl.when(inner)
     def _():
+        for k in range(PLANE):
+            fill_own(k, across)
         whole.wait_recv()
         for k in range(PLANE):
             block(ACROSS, k, across).start()
         for k in range(PLANE):
-            fill(1, k)
+            fill_relay(1, k)
             relayed(RELAY_OUT, k, 1, out_plane).start()
         for k in range(1, PLANE):
-            fill(0, k)
+            fill_relay(0, k)
             relayed(RELAY_OWN, k, 0, plane).start()
-        fill(0, 0)
+        fill_relay(0, 0)
         own_relay.start()
         own_relay.wait()
         for k in range(PLANE):
@@ -343,7 +361,7 @@
     return told[:, :, : asked.shape[1]]
 
 
-def exchange(wanted_all, outgoing, passage_kv):
+def exchange(wanted_all, passage_kv):
     any_space = pl.BlockSpec(memory_space=pl.ANY)
     me, plane, spot = here()
     origin = jnp.where(plane == 2, 0, 3) * PLANE + spot
@@ -358,23 +376,27 @@
         ],
         axis=0,
     )
+    lists = jnp.concatenate([wanted_all[:, me], lists], axis=0)
     lists = jnp.repeat(lists, 2, axis=0).reshape(-1)
+    blocks = (4 * PLANE, cap, 2, PLEN, passage_kv.shape[3] // 2)
     return pl.pallas_call(
         exchange_kernel,
-        out_shape=jax.ShapeDtypeStruct(outgoing.shape, jnp.bfloat16),
-        in_specs=[pl.BlockSpec(memory_space=pltpu.SMEM), any_space, any_space],
+        out_shape=jax.ShapeDtypeStruct(blocks, jnp.bfloat16),
+        in_specs=[pl.BlockSpec(memory_space=pltpu.SMEM), any_space],
         out_specs=any_space,
         scratch_shapes=[
             pltpu.VMEM(passage_kv.shape, jnp.bfloat16),
-            pltpu.VMEM((2, PLANE) + outgoing.shape[1:], jnp.bfloat16),
+            pltpu.VMEM(blocks, jnp.bfloat16),
+            pltpu.VMEM(passage_kv.shape, jnp.bfloat16),
+            pltpu.VMEM((2, PLANE) + blocks[1:], jnp.bfloat16),
             pltpu.SemaphoreType.DMA((7 * PLANE + 1,)),
             pltpu.SemaphoreType.DMA((7 * PLANE + 1,)),
-            pltpu.SemaphoreType.DMA((2,)),
+            pltpu.SemaphoreType.DMA((3,)),
         ],
         compiler_params=pltpu.CompilerParams(
             collective_id=1, has_side_effects=True, vmem_limit_bytes=VMEM_LIMIT
         ),
-    )(lists, outgoing, passage_kv)
+    )(lists, passage_kv)
 
 
 def local(queries, own_keys, own_values, passage_kv, passage_rows, retrieval, offsets):
@@ -394,10 +416,9 @@
     relays = store_count == 8 and head_count == 2 and 2 * cap_dev >= stored_count
     if relays:
         wanted_all = tell(asked, store_count)
-        wanted = jnp.repeat(wanted_all[:, here()[0]], head_count, axis=0)
     else:
         wanted = lax.all_to_all(asked, ("store", "head"), split_axis=0, concat_axis=0, tiled=True)
-    outgoing = pack(wanted, passage_kv, store_count, head_count, cap_dev, CHUNKS)
+        outgoing = pack(wanted, passage_kv, store_count, head_count, cap_dev, CHUNKS)
 
     turn_by = jnp.arange(pick_count, dtype=jnp.int32) % NPASS * PLEN - offsets[pick_ids]
     half_dim = HEAD_DIM // 2
@@ -410,7 +431,7 @@
     result = None
     for chunk in range(CHUNKS):
         if relays:
-            incoming = exchange(wanted_all, outgoing[chunk], passage_kv)
+            incoming = exchange(wanted_all, passage_kv)
         else:
             incoming = lax.all_to_all(
                 outgoing[chunk], ("store", "head"), split_axis=0, concat_axis=0, tiled=True

time: 260 us -> 253 us (0.973)
  Pallas kernels: 250 us -> 243 us
    pallas_call x2 -> x1, Pallas kernels: 217 us -> 210 us  [exchange(): pl.pallas_call(exchange_kernel, out_shape=jax.ShapeDtypeStruct(blocks, jn...]
where the time goes in v6:
time: 253 us; the launch traced here: 251 us
  Pallas kernels  243 us (96%)
  local copies, waits for them, and re-layouts  5.96 us (2%)
    pallas_call x1, Pallas kernels, exchange(): pl.pallas_call(exchange_kernel, out_shape=jax.ShapeDtypeStruct(blocks, jn...  210 us
    pallas_call x1, Pallas kernels, attend(): pl.pallas_call(functools.partial(attend_kernel, group), grid_spec=pltpu.P...  25.6 us
    pallas_call x1, Pallas kernels, tell(): pl.pallas_call(tell_kernel, out_shape=jax.ShapeDtypeStruct((store_count,)...  7.27 us

profile of v6, /device:TPU:15, one launch (start us, length us, event | category | flops | bytes accessed | tf_op | source)
XLA Modules:
  0.0 250.6 jit_solution(16312931976696275704)
XLA Ops:
  0.0 0.0 copy-start
  0.0 0.8 reshape.141
  0.8 0.0 copy-done
  0.8 1.3 gather_fusion.1
  2.1 1.6 gather_fusion
  3.8 0.2 convert_reduce_fusion
  4.0 0.0 copy-start.1
  4.0 0.1 select_reduce_fusion
  4.1 0.1 gather.10
  4.2 0.1 reshape.142
  4.3 0.6 pad.4.asked_ref
  4.9 7.3 %shard_map.73 = s32[8,16,128]{2,1,0:T(8,128)} custom-call(s32[16,128]{1,0:T(8,128)} %pad.4.asked_ref), custom_call_target="tpu_custom_call" | custom-call | tf_op jit(solution)/shard_map/pallas_call | solution.py:353
  12.2 0.8 constant_dynamic-slice_fusion.1
  13.0 0.7 reshape_reshape.3.lists_ref
  13.7 0.3 fusion.1
  14.0 0.8 pad_maximum_fusion
  14.8 210.2 %shard_map.74 = bf16[16,12,2,32,512]{4,3,2,1,0:T(8,128)(2,1)} custom-call(s32[288]{0:T(512)} %reshape_reshape.3.lists_ref, bf16[24,2,32,1024]{3,2,1,0:T(8,128)(2,1)} %kv_ref.1), custom_call_target="tpu_custom_call" | custom-call | tf_op jit(solution)/shard_map/pallas_call | solution.py:382
  225.0 0.0 copy-done.1
  225.0 25.6 %shard_map.75 = bf16[8,64,4096]{2,1,0:T(8,128)(2,1)} custom-call(s32[128]{0:T(128)} %copy-done.1, bf16[8,64,4096]{2,1,0:T(8,128)(2,1)} %q_ref.1, bf16[8,64,512]{2,1,0:T(8,128)(2,1)} %own_k_ref.1, bf16[8,64,512]{2,1,0:T(8,128)(2,1)} %own_v_ref.1, f32[8,16,128]{2,1,0:T(8,128)} %get-tuple-element.14.cos_ref, f32[8,16,128]{2,1,0:T(8,128)} %get-tuple-element.15.sin_ref, ...), custom_call_target="tpu_custom_call" | custom-call | flops 7247757312 | bytes 16777216 | tf_op jit(solution)/shard_map/pallas_call | solution.py:142
  (9 shorter events, 0.1 us)
Async XLA Ops:
  0.0 0.8 copy-start
  4.0 221.0 %copy-start.1 = (s32[128]{0:T(128)}, s32[128]{0:T(128)S(1)}, u32[]{:S(2)}) copy-start(s32[128]{0:T(128)S(1)} %multiply_add_fusion.slot_ref) | copy-start | bytes 1540

commit v7 on v6

--- a/solution.py
+++ b/solution.py
@@ -267,7 +267,8 @@
             fill_own(k, out_plane)
             block(OUT, k, out_plane).start()
             fill_own(k, beyond)
-            block(BEYOND, k, beyond).start()
+            if k < PLANE // 2:
+                block(BEYOND, k, beyond).start()
 
     for k in range(1, PLANE):
         fill_own(k, plane)
@@ -294,6 +295,8 @@
         for k in range(PLANE):
             fill_own(k, across)
         whole.wait_recv()
+        for k in range(PLANE // 2, PLANE):
+            block(BEYOND, k, beyond).start()
         for k in range(PLANE):
             block(ACROSS, k, across).start()
         for k in range(PLANE):

time: 253 us -> 253 us (level)
  no operation moved by 1% of the time
where the time goes in v7:
time: 253 us; the launch traced here: 251 us
  Pallas kernels  243 us (96%)
  local copies, waits for them, and re-layouts  5.96 us (2%)
    pallas_call x1, Pallas kernels, exchange(): pl.pallas_call(exchange_kernel, out_shape=jax.ShapeDtypeStruct(blocks, jn...  210 us
    pallas_call x1, Pallas kernels, attend(): pl.pallas_call(functools.partial(attend_kernel, group), grid_spec=pltpu.P...  25.6 us
    pallas_call x1, Pallas kernels, tell(): pl.pallas_call(tell_kernel, out_shape=jax.ShapeDtypeStruct((store_count,)...  7.27 us

profile of v7, /device:TPU:15, one launch (start us, length us, event | category | flops | bytes accessed | tf_op | source)
XLA Modules:
  0.0 250.6 jit_solution(11939106416818575459)
XLA Ops:
  0.0 0.0 copy-start
  0.0 0.8 reshape.141
  0.8 0.0 copy-done
  0.8 1.3 gather_fusion.1
  2.1 1.6 gather_fusion
  3.8 0.2 convert_reduce_fusion
  4.0 0.0 copy-start.1
  4.0 0.1 select_reduce_fusion
  4.1 0.1 gather.10
  4.2 0.1 reshape.142
  4.3 0.6 pad.4.asked_ref
  4.9 7.3 %shard_map.73 = s32[8,16,128]{2,1,0:T(8,128)} custom-call(s32[16,128]{1,0:T(8,128)} %pad.4.asked_ref), custom_call_target="tpu_custom_call" | custom-call | tf_op jit(solution)/shard_map/pallas_call | solution.py:356
  12.2 0.8 constant_dynamic-slice_fusion.1
  13.0 0.7 reshape_reshape.3.lists_ref
  13.7 0.3 fusion.1
  14.0 0.8 pad_maximum_fusion
  14.8 210.2 %shard_map.74 = bf16[16,12,2,32,512]{4,3,2,1,0:T(8,128)(2,1)} custom-call(s32[288]{0:T(512)} %reshape_reshape.3.lists_ref, bf16[24,2,32,1024]{3,2,1,0:T(8,128)(2,1)} %kv_ref.1), custom_call_target="tpu_custom_call" | custom-call | tf_op jit(solution)/shard_map/pallas_call | solution.py:385
  225.0 0.0 copy-done.1
  225.0 25.6 %shard_map.75 = bf16[8,64,4096]{2,1,0:T(8,128)(2,1)} custom-call(s32[128]{0:T(128)} %copy-done.1, bf16[8,64,4096]{2,1,0:T(8,128)(2,1)} %q_ref.1, bf16[8,64,512]{2,1,0:T(8,128)(2,1)} %own_k_ref.1, bf16[8,64,512]{2,1,0:T(8,128)(2,1)} %own_v_ref.1, f32[8,16,128]{2,1,0:T(8,128)} %get-tuple-element.14.cos_ref, f32[8,16,128]{2,1,0:T(8,128)} %get-tuple-element.15.sin_ref, ...), custom_call_target="tpu_custom_call" | custom-call | flops 7247757312 | bytes 16777216 | tf_op jit(solution)/shard_map/pallas_call | solution.py:142
  (9 shorter events, 0.1 us)
Async XLA Ops:
  0.0 0.8 copy-start
  4.0 221.0 %copy-start.1 = (s32[128]{0:T(128)}, s32[128]{0:T(128)S(1)}, u32[]{:S(2)}) copy-start(s32[128]{0:T(128)S(1)} %multiply_add_fusion.slot_ref) | copy-start | bytes 1540
